TPU v7x, 1024 devices: a whole 4x8x16 slice. The times are simulated.
1024 devices in a mesh: band: 256 (over x, y, z_lo, core), lev: 4 (over z_hi).
Axes of the slice: x: 4, y: 8, z: 16 (z_hi: 4, z_lo: 4; z = z_hi * 4 + z_lo), core: 2. Of those that a mesh axis runs over, the one named last changes fastest.
Arguments:
- spectral: bfloat16 [1280, 2, 4, 3, 1280], P('band', None, 'lev'), may hold values from -0.08984375 to 0.08984375
- legendre: bfloat16 [1280, 256, 1280], P('band'), may hold values from -0.15625 to 0.15625
- level_weights: float32 [4], P('lev'), may hold values from 0.1 to 0.6
- coupling: int32 [1024, 128], P('band'), may hold values from 0 to 131071
- land_sea: int32 [1024, 128], P('band'), may hold values 0 or 1
- spectra: bfloat16 [36, 36, 1024, 128], P('lev', None, 'band'), may hold values from 0.049804688 to 2
- courant: float32 [36], P('lev'), may hold values from 0.1 to 0.65
- growth_rate: float32 [36], P('lev'), may hold values from 0.05 to 0.5
- breaking: float32 [36], P('lev'), may hold values from 0.1 to 1
Outputs:
- grid: float32 [256, 4, 3, 512], P('band', 'lev')
- spectra_out: float32 [36, 36, 1024, 128], P('lev', None, 'band')
- charnock: float32 [1024, 128], P('band')
All inputs are finite; a program needn't handle non-finite values. No bound on the sum of `land_sea` on one device may be relied on, other than what follows from the above.
Results may differ from a plain program's by a relative error of at most 0.0029.
Values may be sent and summed in bfloat16 or wider, within the bound.
A program may use at most 32 MiB of HBM per device.

v0:
```python
import math

import jax
import jax.numpy as jnp
from jax import lax
from jax.sharding import PartitionSpec as P

N = 1280
NLON = 5136
LON_W = 512
LAT_DEV = 1
NF = 36
ND = 36
STEPS = 4


def swapped(block, axis, apart):
    count = lax.axis_size(axis)
    route = []
    for low in range(count):
        high = low | 1 << apart
        if high != low and high < count:
            route += [(low, high), (high, low)]
    return lax.ppermute(block, axis, route)


def padded_2(cells, sides, width):
    for axis, dim in sides:
        count = lax.axis_size(axis)
        ends = count - 1
        head = lax.slice_in_dim(cells, 0, width, axis=dim)
        tail = lax.slice_in_dim(cells, cells.shape[dim] - width, cells.shape[dim], axis=dim)
        cells = jnp.concatenate(
            [
                lax.ppermute(tail, axis, [(i, (i + 1) % count) for i in range(ends)]),
                cells,
                lax.ppermute(head, axis, [((i + 1) % count, i) for i in range(ends)]),
            ],
            axis=dim,
        )
    return cells


def fourier_basis(count):
    waves = jnp.arange(count, dtype=jnp.int32)
    columns = jnp.arange(LON_W, dtype=jnp.int32)
    remains = waves[:, None] * columns[None, :] % NLON
    angles = 2.0 * math.pi / NLON * remains.astype(jnp.float32)
    weights = jnp.where(waves == 0, 1.0, 2.0).astype(jnp.float32)[:, None]
    return jnp.stack([weights * jnp.cos(angles), -weights * jnp.sin(angles)])


def advance(padded, east_speed, north_speed):
    centre = padded[..., 1:-1, :]
    below = padded[..., :-2, :]
    above = padded[..., 2:, :]
    west = jnp.roll(centre, 1, axis=-1)
    east = jnp.roll(centre, -1, axis=-1)
    return (
        centre
        - jnp.maximum(east_speed, 0.0) * (centre - west)
        - jnp.minimum(east_speed, 0.0) * (east - centre)
        - jnp.maximum(north_speed, 0.0) * (centre - below)
        - jnp.minimum(north_speed, 0.0) * (above - centre)
    )


def on_device(
    spectral, legendre, level_weights, coupling, land_sea, spectra, courant, growth_rate, breaking
):
    wave_count = legendre.shape[0]
    window_lats = legendre.shape[1]
    level_count = spectral.shape[2]
    fields = level_count * 3
    band_index = lax.axis_index("band")
    stacked = spectral.reshape(wave_count, 2 * fields, N)
    contract = (((2,), (2,)), ((0,), (0,)))
    band_count = lax.axis_size("band")
    lat_share = window_lats // band_count
    projected = lax.dot_general(stacked, legendre, contract, preferred_element_type=jnp.float32)
    projected = projected.astype(jnp.bfloat16).reshape(wave_count, 2, fields, band_count, lat_share)
    payload = wave_count * 2 * fields * lat_share
    buffer = jnp.transpose(projected, (3, 0, 1, 2, 4)).reshape(band_count, 1, payload)
    bit_count = band_count.bit_length() - 1
    for bit in range(bit_count - 1, -1, -1):
        remaining = buffer.shape[0]
        sources = buffer.shape[1]
        halves = buffer.reshape(2, remaining // 2, sources, payload)
        upper = jnp.right_shift(band_index, bit) % 2 == 1
        keep = jnp.where(upper, halves[1], halves[0])
        outgoing = jnp.where(upper, halves[0], halves[1])
        incoming = swapped(outgoing, "band", bit)
        lower_src = jnp.where(upper, incoming, keep)
        upper_src = jnp.where(upper, keep, incoming)
        buffer = jnp.stack([lower_src, upper_src], axis=2).reshape(
            remaining // 2, sources * 2, payload
        )
    mine = buffer.reshape(band_count * wave_count, 2, fields, lat_share).astype(jnp.float32)
    basis = fourier_basis(band_count * wave_count)
    grid = jnp.einsum("mrfl,rmx->lfx", mine, basis, precision=lax.Precision.HIGHEST)
    grid = grid.reshape(LAT_DEV, level_count, 3, LON_W)
    partial_value = jnp.sum(grid[:, :, 0:2, :] * level_weights[None, :, None, None], axis=1)
    latitude = coupling // LON_W
    longitude = coupling % LON_W
    summed = lax.psum(partial_value, "lev")
    piece = lax.all_gather(summed, "band", axis=0, tiled=True)
    count = piece.shape[0]
    inside = ((latitude >= 0) & (latitude < count)).astype(jnp.float32)
    offset = jnp.clip(latitude, 0, count - 1) * (2 * LON_W) + longitude
    flat = piece.reshape(-1)
    values = jnp.stack([jnp.take(flat, offset), jnp.take(flat, offset + LON_W)])
    wind = values * inside[None]
    freq_count = spectra.shape[0]
    directions = spectra.shape[1]
    theta = 2.0 * math.pi / directions * (jnp.arange(directions).astype(jnp.float32) + 0.5)
    cosines = jnp.cos(theta)[:, None, None]
    sines = jnp.sin(theta)[:, None, None]
    east_speed = courant[:, None, None, None] * cosines[None]
    north_speed = courant[:, None, None, None] * sines[None]
    padded = padded_2(spectra, (("band", 2),), 1).astype(jnp.float32)
    state = advance(padded, east_speed, north_speed)
    for step in range(1, STEPS):
        padded = padded_2(state, (("band", 2),), 1)
        state = advance(padded, east_speed, north_speed)
    wind_east = wind[0]
    wind_north = wind[1]
    push = jnp.maximum(cosines * wind_east[None] + sines * wind_north[None], 0.0)
    landmask = land_sea.astype(jnp.float32)
    growth = growth_rate[:, None, None, None] * push[None]
    result = landmask * state * (1.0 + growth) / (1.0 + breaking[:, None, None, None] * state)
    freq_index = lax.axis_index("lev") * freq_count + jnp.arange(freq_count, dtype=jnp.int32)
    energy = 1.0 + 2.0 * freq_index.astype(jnp.float32) / (NF - 1)
    stress_part = jnp.sum(energy[:, None, None, None] * growth * state, axis=(0, 1)) * landmask
    stress_total = lax.psum(stress_part, "lev")
    stress_mean = stress_total / (NF * ND)
    charnock = 0.011 + 0.5 * stress_mean / (
        stress_mean + 0.05 * (1.0 + wind_east * wind_east + wind_north * wind_north)
    )
    return (grid, result, charnock)


def solution(mesh):
    in_specs = (
        P("band", None, "lev", None, None),
        P("band", None, None),
        P("lev"),
        P("band", None),
        P("band", None),
        P("lev", None, "band", None),
        P("lev"),
        P("lev"),
        P("lev"),
    )
    out_specs = (P("band", "lev", None, None), P("lev", None, "band", None), P("band", None))
    return jax.shard_map(
        on_device, mesh=mesh, in_specs=in_specs, out_specs=out_specs, check_vma=False
    )
```

profile of v0, /device:TPU:1, one launch (start us, length us, event | category | flops | bytes accessed | tf_op | source)
XLA Modules:
  0.0 549.4 jit_solution(15800223871851579560)
XLA Ops:
  10.2 5.5 collective-permute-start
  18.1 12.5 %collective-permute-start.9 = (bf16[9,36,1,128]{3,1,2,0:T(8,128)(2,1)}, bf16[9,36,1,128]{3,1,2,0:T(8,128)(2,1)S(1)}, u32[]{:S(2)}, u32[]{:S(2)}) collective-permute-start(bf16[9,36,1,128]{3,1,2,0:T(8,128)(2,1)} %get-tuple-element.49), channel_id=1, source_target_pairs={{4,0},{8,4},{12,8},{16,12},{20,16},{24,20},{28,24},{32,28},{36,32}... | collective-permute-start | bytes 248840 | tf_op jit(solution)/shard_map/ppermute | solution.py:37
  30.6 1.9 collective-permute-start.8
  32.7 12.2 %sine_multiply_fusion = (f32[1,1280,512]{2,1,0:T(8,128)}, f32[1,1280,512]{2,1,0:T(8,128)}) fusion(f32[1280]{0:T(1024)S(1)} %fusion.63, f32[1280]{0:T(1024)S(1)} %fusion.61), kind=kLoop, calls=%fused_computation.9 | loop fusion | flops 7208960 | bytes 5253120 | tf_op jit(solution)/shard_map/mul | solution.py:50
  45.0 1.9 collective-permute-start.1
  47.0 2.5 collective-permute-done.1
  49.7 1.9 collective-permute-start.2
  51.7 6.7 %collective-permute-done.2 = bf16[32,4,30]{0,1,2:T(4,128)(2,1)} collective-permute-done((bf16[32,4,30]{0,1,2:T(4,128)(2,1)S(1)}, bf16[32,4,30]{0,1,2:T(4,128)(2,1)}, u32[]{:S(2)}, u32[]{:S(2)}) %collective-permute-start.2) | collective-permute-done | bytes 7712 | tf_op jit(solution)/shard_map/ppermute | solution.py:24
  60.0 1.9 collective-permute-start.3
  62.1 3.8 collective-permute-done.3
  66.7 1.9 collective-permute-start.4
  68.7 2.8 collective-permute-done.4
  72.3 1.9 collective-permute-start.5
  74.3 3.7 collective-permute-done.5
  78.8 1.9 collective-permute-start.6
  81.5 2.1 collective-permute-done.6
  84.8 9.9 %collective-permute-start.7 = (bf16[1,128,30]{2,1,0:T(8,128)(2,1)S(1)}, bf16[1,128,30]{2,1,0:T(8,128)(2,1)}, u32[]{:S(2)}, u32[]{:S(2)}) collective-permute-start(bf16[1,128,30]{2,1,0:T(8,128)(2,1)S(1)} %bitcast.110), channel_id=1, source_target_pairs={{0,4},{4,0},{8,12},{12,8},{16,20},{20,16},{24,28},{28,24},{32,36},... | collective-permute-start | bytes 23048 | tf_op jit(solution)/shard_map/ppermute | solution.py:24
  97.8 4.4 fusion.9
  102.8 19.3 %psum.14 = f32[1,2,512]{2,1,0:T(2,128)} all-reduce(f32[1,2,512]{2,1,0:T(2,128)S(1)} %fusion.62), channel_id=1, replica_groups=mesh['band'=256,'lev'=4] {'lev'}, use_global_device_ids=true, to_apply=%region_0.1 | all-reduce | flops 1024 | bytes 8192 | tf_op jit(solution)/shard_map/psum | solution.py:105
  124.9 4.3 collective-permute-start.11
  129.1 1.9 collective-permute-start.10
  132.0 1.5 collective-permute-done.10
  134.3 1.9 collective-permute-start.13
  136.2 4.4 collective-permute-start.12
  144.7 1.9 collective-permute-start.15
  146.6 4.6 collective-permute-start.14
  153.9 354.0 %all-gather.2.cloned.1.call-done = f32[256,2,512]{2,1,0:T(2,128)} async-done(((f32[1,2,512]{2,1,0:T(2,128)}), f32[256,2,512]{2,1,0:T(2,128)}) %all-gather.2.cloned.1.call-update) | async-done | bytes 1048592 | tf_op jit(solution)/shard_map/all_gather | solution.py:106
  507.9 2.5 copy.119
  510.4 6.1 %gather_fusion = f32[512]{0:T(512)S(1)} fusion(f32[262144]{0:T(1024)} %bitcast.97, s32[1024]{0:T(1024)S(1)} %pad_clamp_fusion.1), kind=kCustom, calls=%fused_computation.clone | custom fusion | bytes 6144 | tf_op jit(solution)/shard_map/jit(_take)/gather | solution.py:111
  516.5 6.1 %gather_fusion.1 = f32[512]{0:T(512)S(1)} fusion(f32[262144]{0:T(1024)} %bitcast.98, s32[1024]{0:T(1024)S(1)} %pad_clamp_fusion), kind=kCustom, calls=%fused_computation.1.clone | custom fusion | bytes 6144 | tf_op jit(solution)/shard_map/jit(_take)/gather | solution.py:111
  522.7 3.4 fusion.15
  527.4 14.5 %psum.15 = f32[4,128]{1,0:T(4,128)S(1)} all-reduce(f32[4,128]{1,0:T(4,128)S(1)} %convert_multiply_fusion), channel_id=1, replica_groups=mesh['band'=256,'lev'=4] {'lev'}, use_global_device_ids=true, to_apply=%region_2.4 | all-reduce | flops 512 | bytes 4096 | tf_op jit(solution)/shard_map/psum | solution.py:134
  (105 shorter events, 28.2 us)
Async XLA Ops:
  7.2 2.0 copy-start
  7.2 500.8 %all-gather.2.cloned.1.call-start = ((), (), s32[]{:S(2)}) async-start(), calls=%async_computation | async-start | bytes 1052672 | tf_op jit(solution)/shard_map/all_gather | solution.py:106
  10.2 34.7 %collective-permute-start = (bf16[128,1,30]{0,2,1:T(8,128)(2,1)S(1)}, bf16[128,1,30]{0,2,1:T(8,128)(2,1)S(1)}, u32[]{:S(2)}, u32[]{:S(2)}) collective-permute-start(bf16[128,1,30]{0,2,1:T(8,128)(2,1)S(1)} %select_n.367), channel_id=1, source_target_pairs={{0,512},{512,0},{4,516},{516,4},{8,520},{520,8},{12,524},{524,12},... | collective-permute-start | bytes 23048 | tf_op jit(solution)/shard_map/ppermute | solution.py:24
  16.7 0.7 copy-start.2
  18.1 104.0 %collective-permute-start.9 = (bf16[9,36,1,128]{3,1,2,0:T(8,128)(2,1)}, bf16[9,36,1,128]{3,1,2,0:T(8,128)(2,1)S(1)}, u32[]{:S(2)}, u32[]{:S(2)}) collective-permute-start(bf16[9,36,1,128]{3,1,2,0:T(8,128)(2,1)} %get-tuple-element.49), channel_id=1, source_target_pairs={{4,0},{8,4},{12,8},{16,12},{20,16},{24,20},{28,24},{32,28},{36,32}... | collective-permute-start | bytes 248840 | tf_op jit(solution)/shard_map/ppermute | solution.py:37
  30.6 91.5 %collective-permute-start.8 = (bf16[9,36,1,128]{3,1,2,0:T(8,128)(2,1)}, bf16[9,36,1,128]{3,1,2,0:T(8,128)(2,1)}, u32[]{:S(2)}, u32[]{:S(2)}) collective-permute-start(bf16[9,36,1,128]{3,1,2,0:T(8,128)(2,1)} %get-tuple-element.48), channel_id=1, source_target_pairs={{0,4},{4,8},{8,12},{12,16},{16,20},{20,24},{24,28},{28,32},{32,36}... | collective-permute-start | bytes 248840 | tf_op jit(solution)/shard_map/ppermute | solution.py:35
  32.6 12.2 %copy-start.6 = (f32[9]{0:T(128)S(1)}, f32[9]{0:T(128)}, u32[]{:S(2)}) copy-start(f32[9]{0:T(128)} %param.17) | copy-start | bytes 112
  32.6 14.3 %copy-start.3 = (s32[4,128]{1,0:T(4,128)S(1)}, s32[4,128]{1,0:T(4,128)}, u32[]{:S(2)}) copy-start(s32[4,128]{1,0:T(4,128)} %param.14) | copy-start | bytes 6148
  32.7 48.8 %copy-start.4 = (s32[4,128]{1,0:T(4,128)S(1)}, s32[4,128]{1,0:T(4,128)}, u32[]{:S(2)}) copy-start(s32[4,128]{1,0:T(4,128)} %param.15) | copy-start | bytes 6148
  45.0 4.5 collective-permute-start.1
  49.7 8.7 %collective-permute-start.2 = (bf16[32,4,30]{0,1,2:T(4,128)(2,1)S(1)}, bf16[32,4,30]{0,1,2:T(4,128)(2,1)}, u32[]{:S(2)}, u32[]{:S(2)}) collective-permute-start(bf16[32,4,30]{0,1,2:T(4,128)(2,1)S(1)} %bitcast.114), channel_id=1, source_target_pairs={{0,128},{128,0},{4,132},{132,4},{8,136},{136,8},{12,140},{140,12},... | collective-permute-start | bytes 23048 | tf_op jit(solution)/shard_map/ppermute | solution.py:24
  60.0 5.9 %collective-permute-start.3 = (bf16[16,8,30]{2,0,1:T(8,128)(2,1)}, bf16[16,8,30]{2,0,1:T(8,128)(2,1)}, u32[]{:S(2)}, u32[]{:S(2)}) collective-permute-start(bf16[16,8,30]{2,0,1:T(8,128)(2,1)} %bitcast.109), channel_id=1, source_target_pairs={{0,64},{64,0},{4,68},{68,4},{8,72},{72,8},{12,76},{76,12},{16,80},... | collective-permute-start | bytes 23048 | tf_op jit(solution)/shard_map/ppermute | solution.py:24
  66.7 4.8 collective-permute-start.4
  72.3 5.7 %collective-permute-start.5 = (bf16[4,32,30]{2,1,0:T(8,128)(2,1)S(1)}, bf16[4,32,30]{2,1,0:T(8,128)(2,1)}, u32[]{:S(2)}, u32[]{:S(2)}) collective-permute-start(bf16[4,32,30]{2,1,0:T(8,128)(2,1)S(1)} %bitcast.111), channel_id=1, source_target_pairs={{0,16},{16,0},{4,20},{20,4},{8,24},{24,8},{12,28},{28,12},{32,48},... | collective-permute-start | bytes 23048 | tf_op jit(solution)/shard_map/ppermute | solution.py:24
  78.8 4.8 collective-permute-start.6
  84.8 10.9 %collective-permute-start.7 = (bf16[1,128,30]{2,1,0:T(8,128)(2,1)S(1)}, bf16[1,128,30]{2,1,0:T(8,128)(2,1)}, u32[]{:S(2)}, u32[]{:S(2)}) collective-permute-start(bf16[1,128,30]{2,1,0:T(8,128)(2,1)S(1)} %bitcast.110), channel_id=1, source_target_pairs={{0,4},{4,0},{8,12},{12,8},{16,20},{20,16},{24,28},{28,24},{32,36},... | collective-permute-start | bytes 23048 | tf_op jit(solution)/shard_map/ppermute | solution.py:24
  124.9 7.1 %collective-permute-start.11 = (f32[9,36,1,128]{3,1,2,0:T(8,128)S(1)}, f32[9,36,1,128]{3,1,2,0:T(8,128)S(1)}, u32[]{:S(2)}, u32[]{:S(2)}) collective-permute-start(f32[9,36,1,128]{3,1,2,0:T(8,128)S(1)} %get-tuple-element.47), channel_id=1, source_target_pairs={{4,0},{8,4},{12,8},{16,12},{20,16},{24,20},{28,24},{32,28},{36,32}... | collective-permute-start | bytes 497672 | tf_op jit(solution)/shard_map/ppermute | solution.py:37
  129.1 4.4 collective-permute-start.10
  134.3 7.6 %collective-permute-start.13 = (f32[9,36,1,128]{3,1,2,0:T(8,128)S(1)}, f32[9,36,1,128]{3,1,2,0:T(8,128)S(1)}, u32[]{:S(2)}, u32[]{:S(2)}) collective-permute-start(f32[9,36,1,128]{3,1,2,0:T(8,128)S(1)} %get-tuple-element.41), channel_id=1, source_target_pairs={{4,0},{8,4},{12,8},{16,12},{20,16},{24,20},{28,24},{32,28},{36,32}... | collective-permute-start | bytes 497672 | tf_op jit(solution)/shard_map/ppermute | solution.py:37
  136.2 6.9 %collective-permute-start.12 = (f32[9,36,1,128]{3,1,2,0:T(8,128)S(1)}, f32[9,36,1,128]{3,1,2,0:T(8,128)S(1)}, u32[]{:S(2)}, u32[]{:S(2)}) collective-permute-start(f32[9,36,1,128]{3,1,2,0:T(8,128)S(1)} %get-tuple-element.40), channel_id=1, source_target_pairs={{0,4},{4,8},{8,12},{12,16},{16,20},{20,24},{24,28},{28,32},{32,36}... | collective-permute-start | bytes 497672 | tf_op jit(solution)/shard_map/ppermute | solution.py:35
  143.8 8.7 %copy-start.1 = (f32[9,36,4,128]{3,1,2,0:T(8,128)}, f32[9,36,4,128]{3,1,2,0:T(8,128)S(1)}, u32[]{:S(2)}) copy-start(f32[9,36,4,128]{3,1,2,0:T(8,128)S(1)} %fusion.24) | copy-start | bytes 1990660
  144.7 378.1 %collective-permute-start.15 = (f32[9,36,1,128]{3,1,2,0:T(8,128)}, f32[9,36,1,128]{3,1,2,0:T(8,128)}, u32[]{:S(2)}, u32[]{:S(2)}) collective-permute-start(f32[9,36,1,128]{3,1,2,0:T(8,128)} %get-tuple-element.35), channel_id=1, source_target_pairs={{4,0},{8,4},{12,8},{16,12},{20,16},{24,20},{28,24},{32,28},{36,32}... | collective-permute-start | bytes 497672 | tf_op jit(solution)/shard_map/ppermute | solution.py:37
  146.6 376.1 %collective-permute-start.14 = (f32[9,36,1,128]{3,1,2,0:T(8,128)}, f32[9,36,1,128]{3,1,2,0:T(8,128)}, u32[]{:S(2)}, u32[]{:S(2)}) collective-permute-start(f32[9,36,1,128]{3,1,2,0:T(8,128)} %get-tuple-element.34), channel_id=1, source_target_pairs={{0,4},{4,8},{8,12},{12,16},{16,20},{20,24},{24,28},{28,32},{32,36}... | collective-permute-start | bytes 497672 | tf_op jit(solution)/shard_map/ppermute | solution.py:35
  510.4 12.3 %copy-start.5 = (f32[9]{0:T(128)S(1)}, f32[9]{0:T(128)}, u32[]{:S(2)}) copy-start(f32[9]{0:T(128)} %param.18) | copy-start | bytes 112
  522.6 3.5 copy-start.7
Sparse Core Ops, SparseCore 0:
  122.3 385.5 all-gather.1
where the time goes:
time: 551 us; the launch traced here: 549 us
  waiting for transfers between devices  380 us (69%)
  starting transfers between devices  60.3 us (11%)
  blocking collectives  33.9 us (6%)
  local copies, waits for them, and re-layouts  28.8 us (5%)
  other arithmetic  25.2 us (5%)
  between operations  15.4 us (3%)
    all_gather x1, waiting for transfers between devices, on_device(): piece = lax.all_gather(summed, 'band', axis=0, tiled=True)  354 us
    ppermute x8, starting transfers between devices, swapped(): return lax.ppermute(block, axis, route)  26.9 us
    ppermute x8, waiting for transfers between devices, swapped(): return lax.ppermute(block, axis, route)  22.3 us
    ppermute x4, starting transfers between devices, padded_2(): lax.ppermute(head, axis, [((i + 1) % count, i) for i in range(ends)])  20.6 us
    psum x1, blocking collectives, on_device(): summed = lax.psum(partial_value, 'lev')  19.3 us
    psum x1, blocking collectives, on_device(): stress_total = lax.psum(stress_part, 'lev')  14.5 us
    ppermute x4, starting transfers between devices, padded_2(): lax.ppermute(tail, axis, [(i, (i + 1) % count) for i in range(ends)])  12.8 us
    mul x1, other arithmetic, fourier_basis(): return jnp.stack([weights * jnp.cos(angles), -weights * jnp.sin(angles)])  12.2 us
  transfers between devices with their start and end apart: 17, of which 12 were waited for; matrix products, arithmetic and copies ran while one was open for 9% of the time, Pallas kernels for 0%

commit v1 on v0

v1 whole, which is shorter than its diff:
```python
import math

import jax
import jax.numpy as jnp
from jax import lax
from jax.experimental import pallas as pl
from jax.experimental.pallas import tpu as pltpu
from jax.sharding import PartitionSpec as P

N = 1280
NLON = 5136
LON_W = 512
NLAT = 256
NF = 36
ND = 36
STEPS = 4
NX, NY, NZC, NV = 4, 8, 8, 4
NB = NX * NY * NZC
NR = NX * NZC
NC = NY * NV
MESH = pl.DeviceIdType.MESH
F32, BF16 = jnp.float32, jnp.bfloat16


def turn(t):
    u = (t - jnp.floor(t + 0.5)) * (2.0 * math.pi)
    s = u * u
    even = jnp.full_like(u, 1.0 / math.factorial(16))
    odd = jnp.full_like(u, -1.0 / math.factorial(17 - 2))
    for k in range(7, -1, -1):
        even = even * s + (-1.0) ** k / math.factorial(2 * k)
        if k < 7:
            odd = odd * s + (-1.0) ** k / math.factorial(2 * k + 1)
    return even, u * odd


def cycles(product):
    return (product - jnp.floor(product * (1.0 / NLON)) * NLON) * (1.0 / NLON)


def kernel(
    spec, leg, lw, coup, land, spectra, cour_h, rate_h, brk_h,
    grid_o, out_o, char_o,
    leg_v, spec_v, coup_v, land_v, own_v, s32, proj, send1, recv1, pack, send2, recv2,
    rhs, ebuf, wsend, wrecv, onehot, rsend, rrecv, halo, ext, trig, state, tsum, stsend, strecv, res,
    cour, rate, brk,
    leg_s, in_s, out_s, s1, r1, s2, r2, sw, rw, sr, rr, sh, rh, sc, rc, ss, rs,
):
    b = lax.axis_index("band")
    v = lax.axis_index("lev")
    x = b // 64
    y = lax.rem(b // 8, 8)
    zc = lax.rem(b, 8)
    row = x * NZC + zc
    col = y * NV + v
    up = lax.rem(b + 1, NB)
    down = lax.rem(b + NB - 1, NB)

    def in_row(j):
        return (j // NZC) * (NY * NZC) + y * NZC + lax.rem(j, NZC)

    def in_col(j):
        return x * (NY * NZC) + (j // NV) * NZC + zc

    loads = [pltpu.make_async_copy(leg.at[m], leg_v.at[m], leg_s.at[m]) for m in range(5)]
    spec_c = pltpu.make_async_copy(spec, spec_v, in_s.at[0])
    coup_c = pltpu.make_async_copy(coup, coup_v.at[y], in_s.at[1])
    land_c = pltpu.make_async_copy(land, land_v, in_s.at[2])
    own_c = pltpu.make_async_copy(spectra, own_v, in_s.at[3])
    spec_c.start()
    for c in loads:
        c.start()
    coup_c.start()
    land_c.start()
    own_c.start()
    scalars = [
        pltpu.make_async_copy(h, t, in_s.at[4 + i])
        for i, (h, t) in enumerate(((cour_h, cour), (rate_h, rate), (brk_h, brk)))
    ]
    for c in scalars:
        c.start()

    with jax.named_scope("greet"):
        barrier = pltpu.get_barrier_semaphore()

        def greet_row(j, _):
            t = in_row(lax.rem(row + j, NR))
            pl.semaphore_signal(barrier, inc=1, device_id={"band": t, "lev": v}, device_id_type=MESH)
            return 0

        def greet_col(j, _):
            g = lax.rem(col + j, NC)
            pl.semaphore_signal(
                barrier, inc=1, device_id={"band": in_col(g), "lev": lax.rem(g, NV)}, device_id_type=MESH
            )
            return 0

        lax.fori_loop(1, NR, greet_row, 0)
        lax.fori_loop(1, NC, greet_col, 0)
        pl.semaphore_signal(barrier, inc=1, device_id={"band": up, "lev": v}, device_id_type=MESH)
        pl.semaphore_signal(barrier, inc=1, device_id={"band": down, "lev": v}, device_id_type=MESH)

    with jax.named_scope("tables"):
        slot = lax.broadcasted_iota(jnp.int32, (128, LON_W), 0)
        lon = lax.broadcasted_iota(jnp.int32, (128, LON_W), 1).astype(F32)
        xs = slot >> 5
        slot = slot & 31
        mi = (slot * 43) >> 8
        k = (xs * 320 + mi).astype(F32)
        part = (slot & 1).astype(F32)
        re, im = turn(cycles(k * lon) + 0.25 * part)
        re_hi, im_hi = re.astype(BF16), im.astype(BF16)
        rhs[0:128, 0:LON_W] = re_hi
        rhs[0:128, LON_W:] = im_hi
        rhs[128:256, 0:LON_W] = (re - re_hi.astype(F32)).astype(BF16)
        rhs[128:256, LON_W:] = (im - im_hi.astype(F32)).astype(BF16)
        q = lax.broadcasted_iota(jnp.int32, (64, LON_W), 0).astype(F32)
        lon = lax.broadcasted_iota(jnp.int32, (64, LON_W), 1).astype(F32)
        ec, es = turn(cycles(q * 5.0 * lon))
        ebuf[0] = 2.0 * ec
        ebuf[1] = 2.0 * es
        e = lax.broadcasted_iota(jnp.int32, (18, 8, 128), 0).astype(F32)
        tc, ts = turn((e + 0.5) * (1.0 / ND))
        trig[0] = tc
        trig[1] = ts

    with jax.named_scope("rows"):
        spec_c.wait()
        s32[30:32, :] = jnp.zeros((2, N), F32)
        for j in range(15):
            s32[2 * j : 2 * j + 2, :] = spec_v[j].astype(F32)

    with jax.named_scope("entry_wait"):
        pl.semaphore_wait(barrier, NR - 1 + NC - 1 + 2)

    with jax.named_scope("halo_sends"):
        half = ND // 2
        halo_up = pltpu.make_async_remote_copy(
            src_ref=spectra.at[:, 0:half], dst_ref=halo.at[0], send_sem=sh.at[0], recv_sem=rh.at[0],
            device_id={"band": up, "lev": v}, device_id_type=MESH)
        halo_down = pltpu.make_async_remote_copy(
            src_ref=spectra.at[:, half:], dst_ref=halo.at[1], send_sem=sh.at[1], recv_sem=rh.at[1],
            device_id={"band": down, "lev": v}, device_id_type=MESH)
        halo_up.start()
        halo_down.start()

        def send_coup(j, _):
            t = lax.rem(y + j, NY)
            pltpu.make_async_remote_copy(
                src_ref=coup, dst_ref=coup_v.at[y], send_sem=sc, recv_sem=rc,
                device_id={"band": x * (NY * NZC) + t * NZC + zc, "lev": v}, device_id_type=MESH).start()
            return 0

        lax.fori_loop(1, NY, send_coup, 0)

    with jax.named_scope("legendre"):
        sl = lax.broadcasted_iota(jnp.int32, (128, N), 0)
        held = s32[...]
        held = jnp.concatenate([held, held, held, held], axis=0)
        sx = sl >> 5
        sm = ((sl & 31) * 43) >> 8
        held = jnp.where(sx == x, held, 0.0)
        acc = None
        for m in range(5):
            loads[m].wait()
            s_m = jnp.where(sm == m, held, 0.0).astype(BF16)
            d = lax.dot_general(leg_v[m], s_m, (((1,), (1,)), ((), ())), preferred_element_type=F32)
            acc = d if acc is None else acc + d
        proj[...] = acc.astype(BF16).astype(F32)
        for j in range(NR):
            send1[j] = proj[pl.ds((j // NZC) * 64 + j % NZC, NY, stride=NZC), :]

    with jax.named_scope("first_sends"):
        def send_1(j, _):
            t = lax.rem(row + j, NR)
            pltpu.make_async_remote_copy(
                src_ref=send1.at[t], dst_ref=recv1.at[row], send_sem=s1, recv_sem=r1,
                device_id={"band": in_row(t), "lev": v}, device_id_type=MESH).start()
            return 0

        lax.fori_loop(1, NR, send_1, 0)
        recv1[row] = send1[row]

    with jax.named_scope("onehot_wait"):
        coup_c.wait()
        pltpu.make_async_copy(coup_v.at[0:7], coup_v.at[0:7], rc).wait()
    with jax.named_scope("onehot"):
        lon_i = lax.broadcasted_iota(jnp.int32, (LON_W, 128), 0)

        def hot(g, _):
            for j in range(4):
                point = coup_v[g, pl.ds(j, 1), :] & (LON_W - 1)
                onehot[g * 2 + j // 2, :, (j % 2) * 128 : (j % 2) * 128 + 128] = jnp.where(
                    lon_i == point, 1.0, 0.0).astype(BF16)
            return 0

        lax.fori_loop(0, NY, hot, 0)

    with jax.named_scope("first_wait"):
        pltpu.make_async_copy(recv1.at[0 : NR - 1], recv1.at[0 : NR - 1], r1).wait()
    with jax.named_scope("repack"):
        for z in range(NZC):
            pack[z * 8 : z * 8 + 8, :] = (recv1[z] + recv1[8 + z]) + (recv1[16 + z] + recv1[24 + z])
        for j in range(NY):
            send2[j] = pack[pl.ds(j, NZC, stride=NY), :]

        def send_2(j, _):
            t = lax.rem(y + j, NY)
            pltpu.make_async_remote_copy(
                src_ref=send2.at[t], dst_ref=recv2.at[y], send_sem=s2, recv_sem=r2,
                device_id={"band": x * (NY * NZC) + t * NZC + zc, "lev": v}, device_id_type=MESH).start()
            return 0

        lax.fori_loop(1, NY, send_2, 0)
        recv2[y] = send2[y]

    with jax.named_scope("advection_wait"):
        land_c.wait()
        own_c.wait()
        for c in scalars:
            c.wait()
        halo_up.wait_recv()
        halo_down.wait_recv()
    with jax.named_scope("advection"):
        low = (lax.broadcasted_iota(jnp.int32, (half, 8, 128), 1) < 4)
        land_f = land_v[...].astype(F32)
        land8 = jnp.concatenate([land_f, land_f], axis=0)[None]
        quarter = half // 2
        tsum[...] = jnp.zeros((half, 8, 128), F32)
        first = v * (NF // NV)

        def waves(f, _):
            ext[0, :, 0:4, :] = jnp.where(b == 0, 0.0, halo[0, f].astype(F32))
            ext[0, :, 4:8, :] = own_v[f, 0:half].astype(F32)
            ext[1, :, 0:4, :] = own_v[f, half:].astype(F32)
            ext[1, :, 4:8, :] = jnp.where(b == NB - 1, 0.0, halo[1, f].astype(F32))
            speed = cour[f]
            both = []
            for side in range(2):
                parts = []
                for p in range(2):
                    span = slice(p * quarter, (p + 1) * quarter)
                    s = ext[side, span]
                    a = speed * jnp.abs(trig[0, span])
                    c = speed * trig[1, span]
                    rest = 1.0 - a - c
                    east = 1 if side == p else 127
                    north = 1 if side == 0 else 7
                    for _ in range(STEPS):
                        s = rest * s + a * pltpu.roll(s, east, 2) + c * pltpu.roll(s, north, 1)
                    parts.append(s)
                both.append(jnp.concatenate(parts, axis=0))
            s = jnp.where(low, both[1], both[0])
            energy = 1.0 + 2.0 * (first + f).astype(F32) / (NF - 1)
            tsum[...] += (energy * rate[f]) * s
            state[f] = land8 * s / (1.0 + brk[f] * s)
            return 0

        lax.fori_loop(0, NF // NV, waves, 0)

    with jax.named_scope("second_wait"):
        pltpu.make_async_copy(recv2.at[0 : NY - 1], recv2.at[0 : NY - 1], r2).wait()
    with jax.named_scope("fourier"):
        c = recv2[...].reshape(64, 128)
        lane = lax.broadcasted_iota(jnp.int32, (64, 128), 1)
        line = lax.broadcasted_iota(jnp.int32, (64, 128), 0)
        c = jnp.where((line == 0) & (lane < 6), 0.5 * c, c)
        lane = lane & 31
        field = (lane - 6 * ((lane * 43) >> 8)) >> 1
        lhs = jnp.concatenate([jnp.where(field == f, c, 0.0) for f in range(3)], axis=0).astype(BF16)
        lhs = jnp.concatenate([lhs, lhs], axis=1)
        z = jnp.dot(lhs, rhs[...], preferred_element_type=F32)
        level_weight = lw[0]
        for f in range(3):
            g = jnp.sum(
                z[64 * f : 64 * f + 64, 0:LON_W] * ebuf[0] - z[64 * f : 64 * f + 64, LON_W:] * ebuf[1],
                axis=0, keepdims=True)
            grid_o[0, 0, f : f + 1, :] = g
            if f < 2:
                for j in range(4):
                    wsend[4 * f + j : 4 * f + j + 1, :] = level_weight * g[:, 128 * j : 128 * j + 128]

    with jax.named_scope("wind_sends"):
        def send_w(j, _):
            t = lax.rem(row + j, NR)
            pltpu.make_async_remote_copy(
                src_ref=wsend, dst_ref=wrecv.at[pl.ds(pl.multiple_of(row * 8, 8), 8)], send_sem=sw, recv_sem=rw,
                device_id={"band": in_row(t), "lev": v}, device_id_type=MESH).start()
            return 0

        lax.fori_loop(1, NR, send_w, 0)
        wrecv[pl.ds(pl.multiple_of(row * 8, 8), 8), :] = wsend[...]

    with jax.named_scope("wind_wait"):
        pltpu.make_async_copy(wrecv.at[0 : 8 * NR - 8], wrecv.at[0 : 8 * NR - 8], rw).wait()
    with jax.named_scope("lookup"):
        table = jnp.concatenate(
            [
                jnp.concatenate([wrecv[pl.ds(4 * f + j, NR, stride=8), :] for j in range(4)], axis=1)
                for f in range(2)
            ],
            axis=0,
        )
        t_hi = table.astype(BF16)
    with jax.named_scope("lookup"):
        table = jnp.concatenate([t_hi, (table - t_hi.astype(F32)).astype(BF16)], axis=0)
        ri = lax.broadcasted_iota(jnp.int32, (NR, 128), 0)
        lat = (ri >> 3) * 64 + y * 8 + (ri & 7)

        def look(g, _):
            for h in range(2):
                found = jnp.dot(table, onehot[g * 2 + h], preferred_element_type=F32)
                found = found[0:64] + found[64:128]
                for j in range(2):
                    point = coup_v[g, pl.ds(2 * h + j, 1), :] >> 9
                    mine = lat == point
                    for f in range(2):
                        picked = jnp.where(mine, found[32 * f : 32 * f + 32, 128 * j : 128 * j + 128], 0.0)
                        rsend[g, pl.ds(4 * f + 2 * h + j, 1), :] = jnp.sum(picked, axis=0, keepdims=True)
            return 0

        lax.fori_loop(0, NY, look, 0)

    with jax.named_scope("sum_sends"):
        def send_r(j, _):
            g = lax.rem(col + j, NC)
            pltpu.make_async_remote_copy(
                src_ref=rsend.at[g // NV], dst_ref=rrecv.at[col], send_sem=sr, recv_sem=rr,
                device_id={"band": in_col(g), "lev": lax.rem(g, NV)}, device_id_type=MESH).start()
            return 0

        lax.fori_loop(1, NC, send_r, 0)
        rrecv[col] = rsend[y]
    with jax.named_scope("sum_wait"):
        pltpu.make_async_copy(rrecv.at[0 : NC - 1], rrecv.at[0 : NC - 1], rr).wait()
    with jax.named_scope("stress"):
        wind = jnp.sum(rrecv[...], axis=0)
        turned = pltpu.roll(wind, 4, 0)
        low8 = lax.broadcasted_iota(jnp.int32, (8, 128), 0) < 4
        east8 = jnp.where(low8, -wind, turned)
        north8 = jnp.where(low8, -turned, wind)
        push = jnp.maximum(trig[0] * east8[None] + trig[1] * north8[None], 0.0)
        stress = jnp.sum(push * tsum[...], axis=0)
        stsend[...] = stress + pltpu.roll(stress, 4, 0)

        def send_s(j, _):
            t = lax.rem(v + j, NV)
            pltpu.make_async_remote_copy(
                src_ref=stsend, dst_ref=strecv.at[v], send_sem=ss, recv_sem=rs,
                device_id={"band": b, "lev": t}, device_id_type=MESH).start()
            return 0

        lax.fori_loop(1, NV, send_s, 0)
        strecv[v] = stsend[...]

    with jax.named_scope("result"):
        def result(f, _):
            s = state[f]
            s = s + s * (rate[f] * push)
            res[f, 0:half] = s[:, 4:8, :]
            res[f, half:] = s[:, 0:4, :]
            return 0

        lax.fori_loop(0, NF // NV, result, 0)
        out_c = pltpu.make_async_copy(res, out_o, out_s)
        out_c.start()

    with jax.named_scope("stress_wait"):
        pltpu.make_async_copy(strecv.at[0 : NV - 1], strecv.at[0 : NV - 1], rs).wait()
    with jax.named_scope("charnock"):
        total = (strecv[0] + strecv[1]) + (strecv[2] + strecv[3])
        mean = total * land8[0] * (1.0 / (NF * ND))
        charnock = 0.011 + 0.5 * mean / (mean + 0.05 * (1.0 + wind * wind + turned * turned))
        char_o[...] = charnock[0:4]

    with jax.named_scope("drain"):
        halo_up.wait_send()
        halo_down.wait_send()
        pltpu.make_async_copy(coup_v.at[0:7], coup_v.at[0:7], sc).wait()
        pltpu.make_async_copy(send1.at[0 : NR - 1], send1.at[0 : NR - 1], s1).wait()
        pltpu.make_async_copy(send2.at[0 : NY - 1], send2.at[0 : NY - 1], s2).wait()
        pltpu.make_async_copy(wrecv.at[0 : 8 * NR - 8], wrecv.at[0 : 8 * NR - 8], sw).wait()
        pltpu.make_async_copy(rrecv.at[0 : NC - 1], rrecv.at[0 : NC - 1], sr).wait()
        pltpu.make_async_copy(strecv.at[0 : NV - 1], strecv.at[0 : NV - 1], ss).wait()
        out_c.wait()


def on_device(spectral, legendre, level_weights, coupling, land_sea, spectra, courant, growth_rate, breaking):
    spec = jnp.transpose(spectral, (0, 2, 3, 1, 4)).reshape(15, 2, N)
    any_, vm = (pl.BlockSpec(memory_space=s) for s in (pl.ANY, pltpu.VMEM))
    sm = pltpu.SMEM
    dma = pltpu.SemaphoreType.DMA
    nf, half = NF // NV, ND // 2
    return pl.pallas_call(
        kernel,
        out_shape=(
            jax.ShapeDtypeStruct((1, 1, 3, LON_W), F32),
            jax.ShapeDtypeStruct((nf, ND, 4, 128), F32),
            jax.ShapeDtypeStruct((4, 128), F32),
        ),
        in_specs=[any_, any_, pl.BlockSpec(memory_space=sm)] + [any_] * 6,
        out_specs=(vm, any_, vm),
        scratch_shapes=[
            pltpu.VMEM((5, NLAT, N), BF16),
            pltpu.VMEM((15, 2, N), BF16),
            pltpu.VMEM((NY, 4, 128), jnp.int32),
            pltpu.VMEM((4, 128), jnp.int32),
            pltpu.VMEM((nf, ND, 4, 128), BF16),
            pltpu.VMEM((32, N), F32),
            pltpu.VMEM((NLAT, 128), F32),
            pltpu.VMEM((NR, 8, 128), F32),
            pltpu.VMEM((NR, 8, 128), F32),
            pltpu.VMEM((64, 128), F32),
            pltpu.VMEM((NY, 8, 128), F32),
            pltpu.VMEM((NY, 8, 128), F32),
            pltpu.VMEM((256, 2 * LON_W), BF16),
            pltpu.VMEM((2, 64, LON_W), F32),
            pltpu.VMEM((8, 128), F32),
            pltpu.VMEM((8 * NR, 128), F32),
            pltpu.VMEM((2 * NY, LON_W, 256), BF16),
            pltpu.VMEM((NY, 8, 128), F32),
            pltpu.VMEM((NC, 8, 128), F32),
            pltpu.VMEM((2, nf, half, 4, 128), BF16),
            pltpu.VMEM((2, half, 8, 128), F32),
            pltpu.VMEM((2, half, 8, 128), F32),
            pltpu.VMEM((nf, half, 8, 128), F32),
            pltpu.VMEM((half, 8, 128), F32),
            pltpu.VMEM((8, 128), F32),
            pltpu.VMEM((NV, 8, 128), F32),
            pltpu.VMEM((nf, ND, 4, 128), F32),
            sm((nf,), F32), sm((nf,), F32), sm((nf,), F32),
            dma((5,)), dma((8,)), dma,
            dma, dma, dma, dma, dma, dma, dma, dma,
            dma((2,)), dma((2,)), dma, dma, dma, dma,
        ],
        compiler_params=pltpu.CompilerParams(
            collective_id=0, has_side_effects=True, vmem_limit_bytes=56 * 1024 * 1024
        ),
    )(spec, legendre, level_weights, coupling, land_sea, spectra, courant, growth_rate, breaking)


def solution(mesh):
    in_specs = (
        P("band", None, "lev", None, None),
        P("band", None, None),
        P("lev"),
        P("band", None),
        P("band", None),
        P("lev", None, "band", None),
        P("lev"),
        P("lev"),
        P("lev"),
    )
    out_specs = (P("band", "lev", None, None), P("lev", None, "band", None), P("band", None))
    return jax.shard_map(on_device, mesh=mesh, in_specs=in_specs, out_specs=out_specs, check_vma=False)
```

time: 551 us -> 74.3 us (0.13)
  the two profiles are of different devices: /device:TPU:1 before, /device:TPU:6 now
where the time goes in v1:
time: 74.3 us; the launch traced here: 74 us
  Pallas kernels  68.2 us (92%)
  local copies, waits for them, and re-layouts  4.51 us (6%)
  between operations  1.29 us (2%)
    pallas_call x1, Pallas kernels, on_device(): pl.pallas_call(kernel, out_shape=(jax.ShapeDtypeStruct((1, 1, 3, LON_W),...  68.2 us
    unnamed x2, local copies, waits for them, and re-layouts  3.21 us

profile of v1, /device:TPU:6, one launch (start us, length us, event | category | flops | bytes accessed | tf_op | source)
XLA Modules:
  0.0 74.0 jit_solution(4075343535813387691)
XLA Ops:
  1.3 68.2 %shard_map.112 = (f32[1,1,3,512]{3,2,1,0:T(4,128)}, f32[9,36,4,128]{3,2,1,0:T(4,128)}, f32[4,128]{1,0:T(4,128)}) custom-call(bf16[15,2,1280]{2,1,0:T(2,128)(2,1)} %bitcast.3, bf16[5,256,1280]{2,1,0:T(8,128)(2,1)} %leg.1, f32[1]{0:T(128)S(6)} %copy.15.lw, s32[4,128]{1,0:T(4,128)} %coup.1, s32[4,128]{1,0:T(4,128)} %land.1, bf16[9,36,4,128]{3,2,1,0:T(4,128)(2,1)} %spectra.1, ...), custom_call_target="tpu_custom_call" | custom-call | tf_op jit(solution)/shard_map/pallas_call | solution.py:394
  69.5 1.3 %copy.12 = f32[1,1,3,512]{3,1,2,0:T(1,128)} copy(f32[1,1,3,512]{3,2,1,0:T(4,128)} %get-tuple-element.3) | data formatting | bytes 12288 | tf_op jit(solution)/shard_map/pallas_call | solution.py:394
  70.8 2.0 %copy.16 = f32[9,36,4,128]{3,2,1,0:T(4,128)} copy(f32[9,36,4,128]{3,2,1,0:T(4,128)} %get-tuple-element.10) | data formatting | bytes 1327104
  72.8 1.2 %copy.17 = f32[4,128]{1,0:T(4,128)} copy(f32[4,128]{1,0:T(4,128)} %get-tuple-element.11) | data formatting | bytes 4096

commit v2 on v0

v2 whole, which is shorter than its diff:
```python
import math

import jax
import jax.numpy as jnp
from jax import lax
from jax.experimental import pallas as pl
from jax.experimental.pallas import tpu as pltpu
from jax.sharding import PartitionSpec as P

N = 1280
NLON = 5136
LON_W = 512
NLAT = 256
NF = 36
ND = 36
STEPS = 4
NX, NY, NZC, NV = 4, 8, 8, 4
NB = NX * NY * NZC
NXY = NX * NY
NZ = NV * NZC
HALF = ND // 2
MESH = pl.DeviceIdType.MESH
F32, BF16 = jnp.float32, jnp.bfloat16


def turn(t):
    u = (t - jnp.floor(t + 0.5)) * (2.0 * math.pi)
    s = u * u
    even = jnp.full_like(u, 1.0 / math.factorial(16))
    odd = jnp.full_like(u, -1.0 / math.factorial(17 - 2))
    for k in range(7, -1, -1):
        even = even * s + (-1.0) ** k / math.factorial(2 * k)
        if k < 7:
            odd = odd * s + (-1.0) ** k / math.factorial(2 * k + 1)
    return even, u * odd


def cycles(product):
    return (product - jnp.floor(product * (1.0 / NLON)) * NLON) * (1.0 / NLON)


def plane_offset(x, y, j):
    dy = lax.rem(NY // 2 + ring(j // NX, NY), NY)
    dx = lax.rem(NX // 2 + ring(lax.rem(j, NX), NX), NX)
    return lax.rem(x + dx, NX) * NY + lax.rem(y + dy, NY)


def line_offset(z, j):
    return lax.rem(z + NZ // 2 + ring(j, NZ), NZ)


def ring(j, n):
    k = (j + 1) // 2
    return lax.rem(n + k * (2 * lax.rem(j, 2) - 1), n)


def kernel(
    lw, spec, leg, coup, land, spectra, cour_h, rate_h, brk_h,
    grid_o, out_o, char_o,
    leg_v, spec_v, coup_v, land_v, own_v, s32, proj, recv1, pack, send2, recv2,
    rhs, ebuf, wsend, wrecv, onehot, rsend, rrecv, halo, ext, trig, state, tsum, tsend, trecv,
    cour, rate, brk,
    leg_s, in_s, s1, r1, s2, r2, sw, rw, sr, rr, sh, rh, sc, rc, ss, rs,
):
    b = lax.axis_index("band")
    v = lax.axis_index("lev")
    xy = b // NZC
    x = xy // NY
    y = lax.rem(xy, NY)
    zc = lax.rem(b, NZC)
    zp = v * NZC + zc
    up = lax.rem(b + 1, NB)
    down = lax.rem(b + NB - 1, NB)

    loads = [pltpu.make_async_copy(leg.at[m], leg_v.at[m], leg_s.at[m]) for m in range(5)]
    spec_c = pltpu.make_async_copy(spec, spec_v, in_s.at[0])
    coup_c = pltpu.make_async_copy(coup, coup_v.at[zc], in_s.at[1])
    land_c = pltpu.make_async_copy(land, land_v, in_s.at[2])
    own_c = pltpu.make_async_copy(spectra, own_v, in_s.at[3])
    scalars = [
        pltpu.make_async_copy(h, t, in_s.at[4 + i])
        for i, (h, t) in enumerate(((cour_h, cour), (rate_h, rate), (brk_h, brk)))
    ]
    spec_c.start()
    for c in (*loads, coup_c, land_c, own_c, *scalars):
        c.start()

    barrier = pltpu.get_barrier_semaphore()

    def greet_plane(j, _):
        t = plane_offset(x, y, j)
        pl.semaphore_signal(barrier, inc=1, device_id={"band": t * NZC + zc, "lev": v}, device_id_type=MESH)
        return 0

    def greet_line(j, _):
        t = lax.rem(zp + j, NZ)
        pl.semaphore_signal(
            barrier, inc=1, device_id={"band": xy * NZC + lax.rem(t, NZC), "lev": t // NZC},
            device_id_type=MESH)
        return 0

    lax.fori_loop(0, NXY - 1, greet_plane, 0)
    lax.fori_loop(1, NZ, greet_line, 0)
    pl.semaphore_signal(barrier, inc=1, device_id={"band": up, "lev": v}, device_id_type=MESH)
    pl.semaphore_signal(barrier, inc=1, device_id={"band": down, "lev": v}, device_id_type=MESH)

    spec_c.wait()
    s32[30:32, :] = jnp.zeros((2, N), F32)
    for j in range(15):
        s32[2 * j : 2 * j + 2, :] = spec_v[j].astype(F32)
    sl = lax.broadcasted_iota(jnp.int32, (128, N), 0)
    held = s32[...]
    held = jnp.concatenate([held, held, held, held], axis=0)
    sm = ((sl & 31) * 43) >> 8
    held = jnp.where((sl >> 5) == x, held, 0.0)
    acc = None
    for m in range(5):
        s_m = jnp.where(sm == m, held, 0.0).astype(BF16)
        loads[m].wait()
        d = lax.dot_general(leg_v[m], s_m, (((1,), (1,)), ((), ())), preferred_element_type=F32)
        acc = d if acc is None else acc + d
    proj[...] = acc.astype(BF16).astype(F32).reshape(NXY, 8, 128)

    pl.semaphore_wait(barrier, NXY - 1 + NZ - 1 + 2)

    def send_1(j, _):
        t = plane_offset(x, y, j)
        pltpu.make_async_remote_copy(
            src_ref=proj.at[t], dst_ref=recv1.at[xy], send_sem=s1, recv_sem=r1,
            device_id={"band": t * NZC + zc, "lev": v}, device_id_type=MESH).start()
        return 0

    lax.fori_loop(0, NXY - 1, send_1, 0)
    recv1[xy] = proj[xy]

    halo_up = pltpu.make_async_remote_copy(
        src_ref=spectra.at[:, 0:HALF], dst_ref=halo.at[0], send_sem=sh.at[0], recv_sem=rh.at[0],
        device_id={"band": up, "lev": v}, device_id_type=MESH)
    halo_down = pltpu.make_async_remote_copy(
        src_ref=spectra.at[:, HALF:], dst_ref=halo.at[1], send_sem=sh.at[1], recv_sem=rh.at[1],
        device_id={"band": down, "lev": v}, device_id_type=MESH)

    def send_coup(j, _):
        t = lax.rem(zc + j, NZC)
        pltpu.make_async_remote_copy(
            src_ref=coup, dst_ref=coup_v.at[zc], send_sem=sc, recv_sem=rc,
            device_id={"band": xy * NZC + t, "lev": v}, device_id_type=MESH).start()
        return 0

    lax.fori_loop(1, NZC, send_coup, 0)
    halo_up.start()
    halo_down.start()

    slot = lax.broadcasted_iota(jnp.int32, (128, LON_W), 0)
    lon = lax.broadcasted_iota(jnp.int32, (128, LON_W), 1).astype(F32)
    xs = slot >> 5
    slot = slot & 31
    mi = (slot * 43) >> 8
    k = (xs * 320 + mi).astype(F32)
    part = (slot & 1).astype(F32)
    re, im = turn(cycles(k * lon) + 0.25 * part)
    re_hi, im_hi = re.astype(BF16), im.astype(BF16)
    rhs[0:128, 0:LON_W] = re_hi
    rhs[0:128, LON_W:] = im_hi
    rhs[128:256, 0:LON_W] = (re - re_hi.astype(F32)).astype(BF16)
    rhs[128:256, LON_W:] = (im - im_hi.astype(F32)).astype(BF16)
    q = lax.broadcasted_iota(jnp.int32, (64, LON_W), 0)
    q = ((q & 7) * 8 + (q >> 3)).astype(F32)
    lon = lax.broadcasted_iota(jnp.int32, (64, LON_W), 1).astype(F32)
    ec, es = turn(cycles(q * 5.0 * lon))
    ebuf[0] = 2.0 * ec
    ebuf[1] = 2.0 * es
    e = lax.broadcasted_iota(jnp.int32, (HALF, 8, 128), 0).astype(F32)
    tc, ts = turn((e + 0.5) * (1.0 / ND))
    trig[0] = tc
    trig[1] = ts

    coup_c.wait()
    pltpu.make_async_copy(coup_v.at[0:7], coup_v.at[0:7], rc).wait()
    lon_i = lax.broadcasted_iota(jnp.int32, (LON_W, 128), 0)

    def hot(g, _):
        for j in range(4):
            point = coup_v[g, pl.ds(j, 1), :] & (LON_W - 1)
            onehot[g * 2 + j // 2, :, (j % 2) * 128 : (j % 2) * 128 + 128] = jnp.where(
                lon_i == point, 1.0, 0.0).astype(BF16)
        return 0

    lax.fori_loop(0, NZC, hot, 0)

    pltpu.make_async_copy(recv1.at[0 : NXY - 1], recv1.at[0 : NXY - 1], r1).wait()
    for j in range(NY):
        pack[j * 8 : j * 8 + 8, :] = (recv1[j] + recv1[8 + j]) + (recv1[16 + j] + recv1[24 + j])
    for j in range(NZC):
        send2[j] = pack[pl.ds(j, NY, stride=NZC), :]

    def send_2(j, _):
        t = lax.rem(zc + j, NZC)
        pltpu.make_async_remote_copy(
            src_ref=send2.at[t], dst_ref=recv2.at[zc], send_sem=s2, recv_sem=r2,
            device_id={"band": xy * NZC + t, "lev": v}, device_id_type=MESH).start()
        return 0

    lax.fori_loop(1, NZC, send_2, 0)
    recv2[zc] = send2[zc]

    land_c.wait()
    own_c.wait()
    for c in scalars:
        c.wait()
    halo_up.wait_recv()
    halo_down.wait_recv()
    low = lax.broadcasted_iota(jnp.int32, (HALF, 8, 128), 1) < 4
    land_f = land_v[...].astype(F32)
    land8 = jnp.concatenate([land_f, land_f], axis=0)[None]
    quarter = HALF // 2
    tsum[...] = jnp.zeros((HALF, 8, 128), F32)
    first = v * (NF // NV)

    def waves(f, _):
        ext[0, :, 0:4, :] = jnp.where(b == 0, 0.0, halo[0, f].astype(F32))
        ext[0, :, 4:8, :] = own_v[f, 0:HALF].astype(F32)
        ext[1, :, 0:4, :] = own_v[f, HALF:].astype(F32)
        ext[1, :, 4:8, :] = jnp.where(b == NB - 1, 0.0, halo[1, f].astype(F32))
        speed = cour[f]
        both = []
        for side in range(2):
            parts = []
            for p in range(2):
                span = slice(p * quarter, (p + 1) * quarter)
                s = ext[side, span]
                a = speed * jnp.abs(trig[0, span])
                c = speed * trig[1, span]
                rest = 1.0 - a - c
                east = 1 if side == p else 127
                north = 1 if side == 0 else 7
                for _ in range(STEPS):
                    s = rest * s + a * pltpu.roll(s, east, 2) + c * pltpu.roll(s, north, 1)
                parts.append(s)
            both.append(jnp.concatenate(parts, axis=0))
        s = jnp.where(low, both[1], both[0])
        energy = 1.0 + 2.0 * (first + f).astype(F32) / (NF - 1)
        tsum[...] += (energy * rate[f]) * s
        state[f] = land8 * s / (1.0 + brk[f] * s)
        return 0

    lax.fori_loop(0, NF // NV, waves, 0)
    tsend[...] = tsum[...].reshape(HALF * 8, 128).astype(BF16)

    def send_t(j, _):
        t = lax.rem(v + j, NV)
        pltpu.make_async_remote_copy(
            src_ref=tsend, dst_ref=trecv.at[v], send_sem=ss, recv_sem=rs,
            device_id={"band": b, "lev": t}, device_id_type=MESH).start()
        return 0

    lax.fori_loop(1, NV, send_t, 0)

    pltpu.make_async_copy(recv2.at[0 : NZC - 1], recv2.at[0 : NZC - 1], r2).wait()
    c = recv2[...].reshape(64, 128)
    lane = lax.broadcasted_iota(jnp.int32, (64, 128), 1)
    row = lax.broadcasted_iota(jnp.int32, (64, 128), 0)
    c = jnp.where((row == 0) & (lane < 6), 0.5 * c, c)
    lane = lane & 31
    field = (lane - 6 * ((lane * 43) >> 8)) >> 1
    lhs = jnp.concatenate([jnp.where(field == f, c, 0.0) for f in range(3)], axis=0).astype(BF16)
    lhs = jnp.concatenate([lhs, lhs], axis=1)
    z = jnp.dot(lhs, rhs[...], preferred_element_type=F32)
    level_weight = lw[0]
    for f in range(3):
        g = jnp.sum(
            z[64 * f : 64 * f + 64, 0:LON_W] * ebuf[0] - z[64 * f : 64 * f + 64, LON_W:] * ebuf[1],
            axis=0, keepdims=True)
        grid_o[0, f] = g
        if f < 2:
            for j in range(4):
                wsend[4 * f + j : 4 * f + j + 1, :] = level_weight * g[:, 128 * j : 128 * j + 128]

    def send_w(j, _):
        t = plane_offset(x, y, j)
        pltpu.make_async_remote_copy(
            src_ref=wsend, dst_ref=wrecv.at[pl.ds(pl.multiple_of(xy * 8, 8), 8)], send_sem=sw, recv_sem=rw,
            device_id={"band": t * NZC + zc, "lev": v}, device_id_type=MESH).start()
        return 0

    lax.fori_loop(0, NXY - 1, send_w, 0)
    wrecv[pl.ds(pl.multiple_of(xy * 8, 8), 8), :] = wsend[...]

    pltpu.make_async_copy(wrecv.at[0 : 8 * NXY - 8], wrecv.at[0 : 8 * NXY - 8], rw).wait()
    table = jnp.concatenate(
        [
            jnp.concatenate([wrecv[pl.ds(4 * f + j, NXY, stride=8), :] for j in range(4)], axis=1)
            for f in range(2)
        ],
        axis=0,
    )
    t_hi = table.astype(BF16)
    table = jnp.concatenate([t_hi, (table - t_hi.astype(F32)).astype(BF16)], axis=0)
    lat = lax.broadcasted_iota(jnp.int32, (NXY, 128), 0) * NZC + zc

    def look(g, _):
        for h in range(2):
            found = jnp.dot(table, onehot[g * 2 + h], preferred_element_type=F32)
            found = found[0:64] + found[64:128]
            for j in range(2):
                point = coup_v[g, pl.ds(2 * h + j, 1), :] >> 9
                mine = lat == point
                for f in range(2):
                    picked = jnp.where(mine, found[32 * f : 32 * f + 32, 128 * j : 128 * j + 128], 0.0)
                    rsend[g, pl.ds(4 * f + 2 * h + j, 1), :] = jnp.sum(picked, axis=0, keepdims=True)
        return 0

    lax.fori_loop(0, NZC, look, 0)

    def send_r(j, _):
        t = line_offset(zp, j)
        g = lax.rem(t, NZC)
        pltpu.make_async_remote_copy(
            src_ref=rsend.at[g], dst_ref=rrecv.at[zp], send_sem=sr, recv_sem=rr,
            device_id={"band": xy * NZC + g, "lev": t // NZC}, device_id_type=MESH).start()
        return 0

    lax.fori_loop(0, NZ - 1, send_r, 0)
    rrecv[zp] = rsend[zc]

    pltpu.make_async_copy(trecv.at[0 : NV - 1], trecv.at[0 : NV - 1], rs).wait()
    total = tsum[...]
    for j in range(1, NV):
        total = total + trecv[lax.rem(v + j, NV)].astype(F32).reshape(HALF, 8, 128)
    tsum[...] = total

    pltpu.make_async_copy(rrecv.at[0 : NZ - 1], rrecv.at[0 : NZ - 1], rr).wait()
    wind = jnp.sum(rrecv[...], axis=0)
    turned = pltpu.roll(wind, 4, 0)
    low8 = lax.broadcasted_iota(jnp.int32, (8, 128), 0) < 4
    east8 = jnp.where(low8, -wind, turned)
    north8 = jnp.where(low8, -turned, wind)
    push = jnp.maximum(trig[0] * east8[None] + trig[1] * north8[None], 0.0)
    stress = jnp.sum(push * tsum[...], axis=0)
    mean = (stress + pltpu.roll(stress, 4, 0)) * land8[0] * (1.0 / (NF * ND))
    charnock = 0.011 + 0.5 * mean / (mean + 0.05 * (1.0 + wind * wind + turned * turned))
    char_o[...] = charnock[0:4]

    def result(f, _):
        s = state[f]
        s = s + s * (rate[f] * push)
        out_o[f, 0:HALF] = s[:, 4:8, :]
        out_o[f, HALF:] = s[:, 0:4, :]
        return 0

    lax.fori_loop(0, NF // NV, result, 0)

    halo_up.wait_send()
    halo_down.wait_send()
    pltpu.make_async_copy(coup_v.at[0:7], coup_v.at[0:7], sc).wait()
    pltpu.make_async_copy(recv1.at[0 : NXY - 1], recv1.at[0 : NXY - 1], s1).wait()
    pltpu.make_async_copy(send2.at[0 : NZC - 1], send2.at[0 : NZC - 1], s2).wait()
    pltpu.make_async_copy(wrecv.at[0 : 8 * NXY - 8], wrecv.at[0 : 8 * NXY - 8], sw).wait()
    pltpu.make_async_copy(rrecv.at[0 : NZ - 1], rrecv.at[0 : NZ - 1], sr).wait()
    pltpu.make_async_copy(trecv.at[0 : NV - 1], trecv.at[0 : NV - 1], ss).wait()


def write(grid, out, char, grid_o, out_o, char_o, sems):
    copies = [
        pltpu.make_async_copy(s, d, sems.at[i])
        for i, (s, d) in enumerate(((out, out_o), (grid, grid_o), (char, char_o)))
    ]
    for c in copies:
        c.start()
    for c in copies:
        c.wait()


def on_device(spectral, legendre, level_weights, coupling, land_sea, spectra, courant, growth_rate, breaking):
    spec = jnp.transpose(spectral, (0, 2, 3, 1, 4)).reshape(15, 2, N)
    hbm, vm = (pl.BlockSpec(memory_space=s) for s in (pltpu.HBM, pltpu.VMEM))
    sm = pltpu.SMEM
    dma = pltpu.SemaphoreType.DMA
    nf = NF // NV
    shapes = (
        jax.ShapeDtypeStruct((1, 3, 1, LON_W), F32),
        jax.ShapeDtypeStruct((nf, ND, 4, 128), F32),
        jax.ShapeDtypeStruct((4, 128), F32),
    )
    grid, out, char = pl.pallas_call(
        kernel,
        out_shape=shapes,
        in_specs=[pl.BlockSpec(memory_space=sm)] + [hbm] * 8,
        out_specs=(vm, vm, vm),
        scratch_shapes=[
            pltpu.VMEM((5, NLAT, N), BF16),
            pltpu.VMEM((15, 2, N), BF16),
            pltpu.VMEM((NZC, 4, 128), jnp.int32),
            pltpu.VMEM((4, 128), jnp.int32),
            pltpu.VMEM((nf, ND, 4, 128), BF16),
            pltpu.VMEM((32, N), F32),
            pltpu.VMEM((NXY, 8, 128), F32),
            pltpu.VMEM((NXY, 8, 128), F32),
            pltpu.VMEM((64, 128), F32),
            pltpu.VMEM((NZC, 8, 128), F32),
            pltpu.VMEM((NZC, 8, 128), F32),
            pltpu.VMEM((256, 2 * LON_W), BF16),
            pltpu.VMEM((2, 64, LON_W), F32),
            pltpu.VMEM((8, 128), F32),
            pltpu.VMEM((8 * NXY, 128), F32),
            pltpu.VMEM((2 * NZC, LON_W, 256), BF16),
            pltpu.VMEM((NZC, 8, 128), F32),
            pltpu.VMEM((NZ, 8, 128), F32),
            pltpu.VMEM((2, nf, HALF, 4, 128), BF16),
            pltpu.VMEM((2, HALF, 8, 128), F32),
            pltpu.VMEM((2, HALF, 8, 128), F32),
            pltpu.VMEM((nf, HALF, 8, 128), F32),
            pltpu.VMEM((HALF, 8, 128), F32),
            pltpu.VMEM((HALF * 8, 128), BF16),
            pltpu.VMEM((NV, HALF * 8, 128), BF16),
            sm((nf,), F32), sm((nf,), F32), sm((nf,), F32),
            dma((5,)), dma((8,)),
            dma, dma, dma, dma, dma, dma, dma, dma,
            dma((2,)), dma((2,)), dma, dma, dma, dma,
        ],
        compiler_params=pltpu.CompilerParams(
            collective_id=0, has_side_effects=True, vmem_limit_bytes=40 * 1024 * 1024
        ),
    )(
        level_weights,
        *(
            pltpu.with_memory_space_constraint(a, pltpu.HBM)
            for a in (spec, legendre, coupling, land_sea, spectra, courant, growth_rate, breaking)
        ),
    )
    grid, out, char = pl.pallas_call(
        write,
        out_shape=shapes,
        in_specs=[vm] * 3,
        out_specs=[hbm] * 3,
        scratch_shapes=[dma((3,))],
        compiler_params=pltpu.CompilerParams(vmem_limit_bytes=16 * 1024 * 1024),
    )(grid, out, char)
    return jnp.transpose(grid, (0, 2, 1, 3)), out, char


def solution(mesh):
    in_specs = (
        P("band", None, "lev", None, None),
        P("band", None, None),
        P("lev"),
        P("band", None),
        P("band", None),
        P("lev", None, "band", None),
        P("lev"),
        P("lev"),
        P("lev"),
    )
    out_specs = (P("band", "lev", None, None), P("lev", None, "band", None), P("band", None))
    return jax.shard_map(on_device, mesh=mesh, in_specs=in_specs, out_specs=out_specs, check_vma=False)
```

time: 551 us -> 57.1 us (0.10)
  waiting for transfers between devices: 380 us -> 0 us
  starting transfers between devices: 60.3 us -> 0 us
  Pallas kernels: 0 us -> 55.7 us
  blocking collectives: 33.9 us -> 0 us
  local copies, waits for them, and re-layouts: 28.8 us -> 0 us
  other arithmetic: 25.2 us -> 0 us
  between operations: 15.4 us -> 1.29 us
    all_gather x1 -> x0, waiting for transfers between devices: 354 us -> none  [on_device(): piece = lax.all_gather(summed, 'band', axis=0, tiled=True)]
    ppermute x16 -> x0, starting transfers between devices: 60.3 us -> none  [the longest x8 26.9 us: swapped(): return lax.ppermute(block, axis, route)]
    pallas_call x0 -> x2, Pallas kernels: none -> 55.7 us  [the longest x1 54.8 us: on_device(): pl.pallas_call(kernel, out_shape=shapes, in_specs=[pl.BlockSpec(memory_sp...]
    psum x2 -> x0, blocking collectives: 33.9 us -> none  [the longest x1 19.3 us: on_device(): summed = lax.psum(partial_value, 'lev')]
    ppermute x16 -> x0, waiting for transfers between devices: 26.4 us -> none  [the longest x8 22.3 us: swapped(): return lax.ppermute(block, axis, route)]
    mul x3 -> x0, other arithmetic: 12.2 us -> none  [the longest x1 12.2 us: fourier_basis(): return jnp.stack([weights * jnp.cos(angles), -weights * jnp.sin(angles)])]
    gather x2 -> x0, local copies, waits for them, and re-layouts: 12.1 us -> none  [on_device(): values = jnp.stack([jnp.take(flat, offset), jnp.take(flat, offset + LON_W)])]
    unnamed x21 -> x0, local copies, waits for them, and re-layouts: 7.71 us -> none
  transfers between devices with their start and end apart: 17 -> 0, of which waited for: 12 -> 0; matrix products, arithmetic and copies ran while one was open for 9% -> 0% of each run, Pallas kernels for 0% -> 0%
where the time goes in v2:
time: 57.1 us; the launch traced here: 57 us
  Pallas kernels  55.7 us (98%)
  between operations  1.29 us (2%)
    pallas_call x1, Pallas kernels, on_device(): pl.pallas_call(kernel, out_shape=shapes, in_specs=[pl.BlockSpec(memory_sp...  54.8 us

profile of v2, /device:TPU:1, one launch (start us, length us, event | category | flops | bytes accessed | tf_op | source)
XLA Modules:
  0.0 57.0 jit_solution(7525507686629081355)
XLA Ops:
  1.3 54.8 %shard_map.112 = (f32[1,3,1,512]{3,2,1,0:T(1,128)S(1)}, f32[9,36,4,128]{3,2,1,0:T(4,128)S(1)}, f32[4,128]{1,0:T(4,128)S(1)}) custom-call(f32[1]{0:T(128)S(6)} %copy.13.lw, bf16[15,2,1280]{2,1,0:T(2,128)(2,1)} %bitcast.6, bf16[5,256,1280]{2,1,0:T(8,128)(2,1)} %leg.1, s32[4,128]{1,0:T(4,128)} %coup.1, s32[4,128]{1,0:T(4,128)} %land.1, ...), custom_call_target="tpu_custom_call" | custom-call | tf_op jit(solution)/shard_map/pallas_call | solution.py:385
  56.1 0.9 %shard_map.113 = (f32[1,3,1,512]{3,2,1,0:T(1,128)}, f32[9,36,4,128]{3,2,1,0:T(4,128)}, f32[4,128]{1,0:T(4,128)}) custom-call(f32[1,3,1,512]{3,2,1,0:T(1,128)S(1)} %get-tuple-element.9.grid, f32[9,36,4,128]{3,2,1,0:T(4,128)S(1)} %get-tuple-element.10.out, f32[4,128]{1,0:T(4,128)S(1)} %get-tuple-element.11.char), custom_call_target="tpu_custom_call" | custom-call | tf_op jit(solution)/shard_map/pallas_call | solution.py:431

commit v3 on v2

--- a/solution.py
+++ b/solution.py
@@ -39,26 +39,27 @@
     return (product - jnp.floor(product * (1.0 / NLON)) * NLON) * (1.0 / NLON)
 
 
-def plane_offset(x, y, j):
-    dy = lax.rem(NY // 2 + ring(j // NX, NY), NY)
-    dx = lax.rem(NX // 2 + ring(lax.rem(j, NX), NX), NX)
-    return lax.rem(x + dx, NX) * NY + lax.rem(y + dy, NY)
-
-
-def line_offset(z, j):
-    return lax.rem(z + NZ // 2 + ring(j, NZ), NZ)
-
-
-def ring(j, n):
-    k = (j + 1) // 2
-    return lax.rem(n + k * (2 * lax.rem(j, 2) - 1), n)
+def plane_partners(x, y):
+    xs = [lax.rem(x + d, NX) * NY for d in (2, 3, 1, 0)]
+    for dy in (4, 5, 3, 6, 2, 7, 1, 0):
+        yy = lax.rem(y + dy, NY)
+        for xx in xs[: 4 if dy else 3]:
+            yield xx + yy
+
+
+def line_partners(v, zc):
+    vs = [lax.rem(v + d, NV) for d in (2, 1, 3, 0)]
+    zs = [lax.rem(zc + d, NZC) for d in range(NZC)]
+    for i, vv in enumerate(vs):
+        for zz in zs[1 if i == 3 else 0 :]:
+            yield vv, zz
 
 
 def kernel(
     lw, spec, leg, coup, land, spectra, cour_h, rate_h, brk_h,
     grid_o, out_o, char_o,
     leg_v, spec_v, coup_v, land_v, own_v, s32, proj, recv1, pack, send2, recv2,
-    rhs, ebuf, wsend, wrecv, onehot, rsend, rrecv, halo, ext, trig, state, tsum, tsend, trecv,
+    rhs, ebuf, wrow, wsend, wrecv, wtab, onehot, rrow, rsend, rrecv, halo, ext, trig, state, tsum, tsend, trecv,
     cour, rate, brk,
     leg_s, in_s, s1, r1, s2, r2, sw, rw, sr, rr, sh, rh, sc, rc, ss, rs,
 ):
@@ -87,20 +88,11 @@
 
     barrier = pltpu.get_barrier_semaphore()
 
-    def greet_plane(j, _):
-        t = plane_offset(x, y, j)
+    for vv, zz in line_partners(v, zc):
+        pl.semaphore_signal(
+            barrier, inc=1, device_id={"band": xy * NZC + zz, "lev": vv}, device_id_type=MESH)
+    for t in plane_partners(x, y):
         pl.semaphore_signal(barrier, inc=1, device_id={"band": t * NZC + zc, "lev": v}, device_id_type=MESH)
-        return 0
-
-    def greet_line(j, _):
-        t = lax.rem(zp + j, NZ)
-        pl.semaphore_signal(
-            barrier, inc=1, device_id={"band": xy * NZC + lax.rem(t, NZC), "lev": t // NZC},
-            device_id_type=MESH)
-        return 0
-
-    lax.fori_loop(0, NXY - 1, greet_plane, 0)
-    lax.fori_loop(1, NZ, greet_line, 0)
     pl.semaphore_signal(barrier, inc=1, device_id={"band": up, "lev": v}, device_id_type=MESH)
     pl.semaphore_signal(barrier, inc=1, device_id={"band": down, "lev": v}, device_id_type=MESH)
 
@@ -119,18 +111,14 @@
         loads[m].wait()
         d = lax.dot_general(leg_v[m], s_m, (((1,), (1,)), ((), ())), preferred_element_type=F32)
         acc = d if acc is None else acc + d
-    proj[...] = acc.astype(BF16).astype(F32).reshape(NXY, 8, 128)
+    proj[...] = acc.reshape(NXY, 8, 128).astype(BF16)
 
     pl.semaphore_wait(barrier, NXY - 1 + NZ - 1 + 2)
 
-    def send_1(j, _):
-        t = plane_offset(x, y, j)
+    for t in plane_partners(x, y):
         pltpu.make_async_remote_copy(
             src_ref=proj.at[t], dst_ref=recv1.at[xy], send_sem=s1, recv_sem=r1,
             device_id={"band": t * NZC + zc, "lev": v}, device_id_type=MESH).start()
-        return 0
-
-    lax.fori_loop(0, NXY - 1, send_1, 0)
     recv1[xy] = proj[xy]
 
     halo_up = pltpu.make_async_remote_copy(
@@ -190,18 +178,16 @@
 
     pltpu.make_async_copy(recv1.at[0 : NXY - 1], recv1.at[0 : NXY - 1], r1).wait()
     for j in range(NY):
-        pack[j * 8 : j * 8 + 8, :] = (recv1[j] + recv1[8 + j]) + (recv1[16 + j] + recv1[24 + j])
+        parts = [recv1[8 * i + j].astype(F32) for i in range(NX)]
+        pack[j * 8 : j * 8 + 8, :] = (parts[0] + parts[1]) + (parts[2] + parts[3])
     for j in range(NZC):
-        send2[j] = pack[pl.ds(j, NY, stride=NZC), :]
-
-    def send_2(j, _):
+        send2[j] = pack[pl.ds(j, NY, stride=NZC), :].astype(BF16)
+
+    for j in (4, 3, 5, 2, 6, 1, 7):
         t = lax.rem(zc + j, NZC)
         pltpu.make_async_remote_copy(
             src_ref=send2.at[t], dst_ref=recv2.at[zc], send_sem=s2, recv_sem=r2,
             device_id={"band": xy * NZC + t, "lev": v}, device_id_type=MESH).start()
-        return 0
-
-    lax.fori_loop(1, NZC, send_2, 0)
     recv2[zc] = send2[zc]
 
     land_c.wait()
@@ -257,7 +243,7 @@
     lax.fori_loop(1, NV, send_t, 0)
 
     pltpu.make_async_copy(recv2.at[0 : NZC - 1], recv2.at[0 : NZC - 1], r2).wait()
-    c = recv2[...].reshape(64, 128)
+    c = recv2[...].astype(F32).reshape(64, 128)
     lane = lax.broadcasted_iota(jnp.int32, (64, 128), 1)
     row = lax.broadcasted_iota(jnp.int32, (64, 128), 0)
     c = jnp.where((row == 0) & (lane < 6), 0.5 * c, c)
@@ -274,53 +260,42 @@
         grid_o[0, f] = g
         if f < 2:
             for j in range(4):
-                wsend[4 * f + j : 4 * f + j + 1, :] = level_weight * g[:, 128 * j : 128 * j + 128]
-
-    def send_w(j, _):
-        t = plane_offset(x, y, j)
+                wrow[4 * f + j : 4 * f + j + 1, :] = level_weight * g[:, 128 * j : 128 * j + 128]
+
+    wsend[...] = wrow[...].astype(BF16)
+    for t in plane_partners(x, y):
         pltpu.make_async_remote_copy(
-            src_ref=wsend, dst_ref=wrecv.at[pl.ds(pl.multiple_of(xy * 8, 8), 8)], send_sem=sw, recv_sem=rw,
+            src_ref=wsend, dst_ref=wrecv.at[xy], send_sem=sw, recv_sem=rw,
             device_id={"band": t * NZC + zc, "lev": v}, device_id_type=MESH).start()
-        return 0
-
-    lax.fori_loop(0, NXY - 1, send_w, 0)
-    wrecv[pl.ds(pl.multiple_of(xy * 8, 8), 8), :] = wsend[...]
-
-    pltpu.make_async_copy(wrecv.at[0 : 8 * NXY - 8], wrecv.at[0 : 8 * NXY - 8], rw).wait()
+    wrecv[xy] = wsend[...]
+
+    pltpu.make_async_copy(wrecv.at[0 : NXY - 1], wrecv.at[0 : NXY - 1], rw).wait()
+    wtab[...] = wrecv[...].astype(F32).reshape(8 * NXY, 128)
     table = jnp.concatenate(
         [
-            jnp.concatenate([wrecv[pl.ds(4 * f + j, NXY, stride=8), :] for j in range(4)], axis=1)
+            jnp.concatenate([wtab[pl.ds(4 * f + j, NXY, stride=8), :] for j in range(4)], axis=1)
             for f in range(2)
         ],
         axis=0,
-    )
-    t_hi = table.astype(BF16)
-    table = jnp.concatenate([t_hi, (table - t_hi.astype(F32)).astype(BF16)], axis=0)
+    ).astype(BF16)
     lat = lax.broadcasted_iota(jnp.int32, (NXY, 128), 0) * NZC + zc
-
-    def look(g, _):
+    others = [lax.rem(v + d, NV) for d in (2, 1, 3, 0)]
+    for i in range(NZC):
+        g = lax.rem(zc + i, NZC)
         for h in range(2):
             found = jnp.dot(table, onehot[g * 2 + h], preferred_element_type=F32)
-            found = found[0:64] + found[64:128]
             for j in range(2):
                 point = coup_v[g, pl.ds(2 * h + j, 1), :] >> 9
                 mine = lat == point
                 for f in range(2):
                     picked = jnp.where(mine, found[32 * f : 32 * f + 32, 128 * j : 128 * j + 128], 0.0)
-                    rsend[g, pl.ds(4 * f + 2 * h + j, 1), :] = jnp.sum(picked, axis=0, keepdims=True)
-        return 0
-
-    lax.fori_loop(0, NZC, look, 0)
-
-    def send_r(j, _):
-        t = line_offset(zp, j)
-        g = lax.rem(t, NZC)
-        pltpu.make_async_remote_copy(
-            src_ref=rsend.at[g], dst_ref=rrecv.at[zp], send_sem=sr, recv_sem=rr,
-            device_id={"band": xy * NZC + g, "lev": t // NZC}, device_id_type=MESH).start()
-        return 0
-
-    lax.fori_loop(0, NZ - 1, send_r, 0)
+                    line = 4 * f + 2 * h + j
+                    rrow[i, line : line + 1, :] = jnp.sum(picked, axis=0, keepdims=True)
+        rsend[g] = rrow[i].astype(BF16)
+        for vv in others[: 4 if i else 3]:
+            pltpu.make_async_remote_copy(
+                src_ref=rsend.at[g], dst_ref=rrecv.at[zp], send_sem=sr, recv_sem=rr,
+                device_id={"band": xy * NZC + g, "lev": vv}, device_id_type=MESH).start()
     rrecv[zp] = rsend[zc]
 
     pltpu.make_async_copy(trecv.at[0 : NV - 1], trecv.at[0 : NV - 1], rs).wait()
@@ -330,7 +305,7 @@
     tsum[...] = total
 
     pltpu.make_async_copy(rrecv.at[0 : NZ - 1], rrecv.at[0 : NZ - 1], rr).wait()
-    wind = jnp.sum(rrecv[...], axis=0)
+    wind = jnp.sum(rrecv[...].astype(F32), axis=0)
     turned = pltpu.roll(wind, 4, 0)
     low8 = lax.broadcasted_iota(jnp.int32, (8, 128), 0) < 4
     east8 = jnp.where(low8, -wind, turned)
@@ -355,15 +330,16 @@
     pltpu.make_async_copy(coup_v.at[0:7], coup_v.at[0:7], sc).wait()
     pltpu.make_async_copy(recv1.at[0 : NXY - 1], recv1.at[0 : NXY - 1], s1).wait()
     pltpu.make_async_copy(send2.at[0 : NZC - 1], send2.at[0 : NZC - 1], s2).wait()
-    pltpu.make_async_copy(wrecv.at[0 : 8 * NXY - 8], wrecv.at[0 : 8 * NXY - 8], sw).wait()
+    pltpu.make_async_copy(wrecv.at[0 : NXY - 1], wrecv.at[0 : NXY - 1], sw).wait()
     pltpu.make_async_copy(rrecv.at[0 : NZ - 1], rrecv.at[0 : NZ - 1], sr).wait()
     pltpu.make_async_copy(trecv.at[0 : NV - 1], trecv.at[0 : NV - 1], ss).wait()
 
 
 def write(grid, out, char, grid_o, out_o, char_o, sems):
+    pieces = [(out.at[i : i + 3], out_o.at[i : i + 3]) for i in range(0, NF // NV, 3)]
     copies = [
         pltpu.make_async_copy(s, d, sems.at[i])
-        for i, (s, d) in enumerate(((out, out_o), (grid, grid_o), (char, char_o)))
+        for i, (s, d) in enumerate((*pieces, (grid, grid_o), (char, char_o)))
     ]
     for c in copies:
         c.start()
@@ -394,18 +370,21 @@
             pltpu.VMEM((4, 128), jnp.int32),
             pltpu.VMEM((nf, ND, 4, 128), BF16),
             pltpu.VMEM((32, N), F32),
-            pltpu.VMEM((NXY, 8, 128), F32),
-            pltpu.VMEM((NXY, 8, 128), F32),
+            pltpu.VMEM((NXY, 8, 128), BF16),
+            pltpu.VMEM((NXY, 8, 128), BF16),
             pltpu.VMEM((64, 128), F32),
-            pltpu.VMEM((NZC, 8, 128), F32),
-            pltpu.VMEM((NZC, 8, 128), F32),
+            pltpu.VMEM((NZC, 8, 128), BF16),
+            pltpu.VMEM((NZC, 8, 128), BF16),
             pltpu.VMEM((256, 2 * LON_W), BF16),
             pltpu.VMEM((2, 64, LON_W), F32),
             pltpu.VMEM((8, 128), F32),
+            pltpu.VMEM((8, 128), BF16),
+            pltpu.VMEM((NXY, 8, 128), BF16),
             pltpu.VMEM((8 * NXY, 128), F32),
             pltpu.VMEM((2 * NZC, LON_W, 256), BF16),
             pltpu.VMEM((NZC, 8, 128), F32),
-            pltpu.VMEM((NZ, 8, 128), F32),
+            pltpu.VMEM((NZC, 8, 128), BF16),
+            pltpu.VMEM((NZ, 8, 128), BF16),
             pltpu.VMEM((2, nf, HALF, 4, 128), BF16),
             pltpu.VMEM((2, HALF, 8, 128), F32),
             pltpu.VMEM((2, HALF, 8, 128), F32),
@@ -433,7 +412,7 @@
         out_shape=shapes,
         in_specs=[vm] * 3,
         out_specs=[hbm] * 3,
-        scratch_shapes=[dma((3,))],
+        scratch_shapes=[dma((5,))],
         compiler_params=pltpu.CompilerParams(vmem_limit_bytes=16 * 1024 * 1024),
     )(grid, out, char)
     return jnp.transpose(grid, (0, 2, 1, 3)), out, char

time: 57.1 us -> 51.7 us (0.905)
  Pallas kernels: 55.7 us -> 50.3 us
    pallas_call x1, Pallas kernels: 54.8 us -> 49.4 us  [on_device(): pl.pallas_call(kernel, out_shape=shapes, in_specs=[pl.BlockSpec(memory_sp...]
where the time goes in v3:
time: 51.7 us; the launch traced here: 51.5 us
  Pallas kernels  50.3 us (97%)
  between operations  1.29 us (2%)
    pallas_call x1, Pallas kernels, on_device(): pl.pallas_call(kernel, out_shape=shapes, in_specs=[pl.BlockSpec(memory_sp...  49.4 us

profile of v3, /device:TPU:1, one launch (start us, length us, event | category | flops | bytes accessed | tf_op | source)
XLA Modules:
  0.0 51.5 jit_solution(9564936650591861376)
XLA Ops:
  1.3 49.4 %shard_map.112 = (f32[1,3,1,512]{3,2,1,0:T(1,128)S(1)}, f32[9,36,4,128]{3,2,1,0:T(4,128)S(1)}, f32[4,128]{1,0:T(4,128)S(1)}) custom-call(f32[1]{0:T(128)S(6)} %copy.13.lw, bf16[15,2,1280]{2,1,0:T(2,128)(2,1)} %bitcast.6, bf16[5,256,1280]{2,1,0:T(8,128)(2,1)} %leg.1, s32[4,128]{1,0:T(4,128)} %coup.1, s32[4,128]{1,0:T(4,128)} %land.1, ...), custom_call_target="tpu_custom_call" | custom-call | tf_op jit(solution)/shard_map/pallas_call | solution.py:361
  50.7 0.9 %shard_map.113 = (f32[1,3,1,512]{3,2,1,0:T(1,128)}, f32[9,36,4,128]{3,2,1,0:T(4,128)}, f32[4,128]{1,0:T(4,128)}) custom-call(f32[1,3,1,512]{3,2,1,0:T(1,128)S(1)} %get-tuple-element.9.grid, f32[9,36,4,128]{3,2,1,0:T(4,128)S(1)} %get-tuple-element.10.out, f32[4,128]{1,0:T(4,128)S(1)} %get-tuple-element.11.char), custom_call_target="tpu_custom_call" | custom-call | tf_op jit(solution)/shard_map/pallas_call | solution.py:410

commit v4 on v3

--- a/solution.py
+++ b/solution.py
@@ -47,21 +47,13 @@
             yield xx + yy
 
 
-def line_partners(v, zc):
-    vs = [lax.rem(v + d, NV) for d in (2, 1, 3, 0)]
-    zs = [lax.rem(zc + d, NZC) for d in range(NZC)]
-    for i, vv in enumerate(vs):
-        for zz in zs[1 if i == 3 else 0 :]:
-            yield vv, zz
-
-
 def kernel(
     lw, spec, leg, coup, land, spectra, cour_h, rate_h, brk_h,
     grid_o, out_o, char_o,
     leg_v, spec_v, coup_v, land_v, own_v, s32, proj, recv1, pack, send2, recv2,
     rhs, ebuf, wrow, wsend, wrecv, wtab, onehot, rrow, rsend, rrecv, halo, ext, trig, state, tsum, tsend, trecv,
     cour, rate, brk,
-    leg_s, in_s, s1, r1, s2, r2, sw, rw, sr, rr, sh, rh, sc, rc, ss, rs,
+    leg_s, in_s, s1, r1, s2, r2, sw, rw, sr, rr, sh, rh, sc, rc, ss, rs, heard, told,
 ):
     b = lax.axis_index("band")
     v = lax.axis_index("lev")
@@ -82,19 +74,22 @@
         pltpu.make_async_copy(h, t, in_s.at[4 + i])
         for i, (h, t) in enumerate(((cour_h, cour), (rate_h, rate), (brk_h, brk)))
     ]
+    barrier = pltpu.get_barrier_semaphore()
+
+    for t in plane_partners(x, y):
+        pl.semaphore_signal(barrier, inc=1, device_id={"band": t * NZC + zc, "lev": v}, device_id_type=MESH)
+    near = [lax.rem(v + d, NV) for d in (1, NV - 1)]
+    for vv in near:
+        pl.semaphore_signal(barrier, inc=1, device_id={"band": b, "lev": vv}, device_id_type=MESH)
+    mates = [xy * NZC + lax.rem(zc + d, NZC) for d in (4, 3, 5, 2, 6, 1, 7)]
+    for t in mates:
+        pl.semaphore_signal(barrier, inc=1, device_id={"band": t, "lev": v}, device_id_type=MESH)
+    pl.semaphore_signal(barrier, inc=1, device_id={"band": up, "lev": v}, device_id_type=MESH)
+    pl.semaphore_signal(barrier, inc=1, device_id={"band": down, "lev": v}, device_id_type=MESH)
+
     spec_c.start()
     for c in (*loads, coup_c, land_c, own_c, *scalars):
         c.start()
-
-    barrier = pltpu.get_barrier_semaphore()
-
-    for vv, zz in line_partners(v, zc):
-        pl.semaphore_signal(
-            barrier, inc=1, device_id={"band": xy * NZC + zz, "lev": vv}, device_id_type=MESH)
-    for t in plane_partners(x, y):
-        pl.semaphore_signal(barrier, inc=1, device_id={"band": t * NZC + zc, "lev": v}, device_id_type=MESH)
-    pl.semaphore_signal(barrier, inc=1, device_id={"band": up, "lev": v}, device_id_type=MESH)
-    pl.semaphore_signal(barrier, inc=1, device_id={"band": down, "lev": v}, device_id_type=MESH)
 
     spec_c.wait()
     s32[30:32, :] = jnp.zeros((2, N), F32)
@@ -113,13 +108,16 @@
         acc = d if acc is None else acc + d
     proj[...] = acc.reshape(NXY, 8, 128).astype(BF16)
 
-    pl.semaphore_wait(barrier, NXY - 1 + NZ - 1 + 2)
+    pl.semaphore_wait(barrier, NXY - 1 + 2 + NZC - 1 + 2)
 
     for t in plane_partners(x, y):
         pltpu.make_async_remote_copy(
             src_ref=proj.at[t], dst_ref=recv1.at[xy], send_sem=s1, recv_sem=r1,
             device_id={"band": t * NZC + zc, "lev": v}, device_id_type=MESH).start()
     recv1[xy] = proj[xy]
+
+    for vv in near:
+        pl.semaphore_signal(heard, inc=1, device_id={"band": b, "lev": vv}, device_id_type=MESH)
 
     halo_up = pltpu.make_async_remote_copy(
         src_ref=spectra.at[:, 0:HALF], dst_ref=halo.at[0], send_sem=sh.at[0], recv_sem=rh.at[0],
@@ -189,6 +187,10 @@
             src_ref=send2.at[t], dst_ref=recv2.at[zc], send_sem=s2, recv_sem=r2,
             device_id={"band": xy * NZC + t, "lev": v}, device_id_type=MESH).start()
     recv2[zc] = send2[zc]
+
+    pl.semaphore_wait(heard, 2)
+    for t in mates:
+        pl.semaphore_signal(told, inc=1, device_id={"band": t, "lev": v}, device_id_type=MESH)
 
     land_c.wait()
     own_c.wait()
@@ -249,25 +251,30 @@
     c = jnp.where((row == 0) & (lane < 6), 0.5 * c, c)
     lane = lane & 31
     field = (lane - 6 * ((lane * 43) >> 8)) >> 1
-    lhs = jnp.concatenate([jnp.where(field == f, c, 0.0) for f in range(3)], axis=0).astype(BF16)
-    lhs = jnp.concatenate([lhs, lhs], axis=1)
-    z = jnp.dot(lhs, rhs[...], preferred_element_type=F32)
     level_weight = lw[0]
-    for f in range(3):
-        g = jnp.sum(
-            z[64 * f : 64 * f + 64, 0:LON_W] * ebuf[0] - z[64 * f : 64 * f + 64, LON_W:] * ebuf[1],
-            axis=0, keepdims=True)
-        grid_o[0, f] = g
-        if f < 2:
-            for j in range(4):
-                wrow[4 * f + j : 4 * f + j + 1, :] = level_weight * g[:, 128 * j : 128 * j + 128]
-
+
+    def synthesis(fields):
+        lhs = jnp.concatenate([jnp.where(field == f, c, 0.0) for f in fields], axis=0).astype(BF16)
+        z = jnp.dot(jnp.concatenate([lhs, lhs], axis=1), rhs[...], preferred_element_type=F32)
+        return [
+            jnp.sum(
+                z[64 * i : 64 * i + 64, 0:LON_W] * ebuf[0] - z[64 * i : 64 * i + 64, LON_W:] * ebuf[1],
+                axis=0, keepdims=True)
+            for i in range(len(fields))
+        ]
+
+    winds = synthesis((0, 1))
+    for f in range(2):
+        for j in range(4):
+            wrow[4 * f + j : 4 * f + j + 1, :] = level_weight * winds[f][:, 128 * j : 128 * j + 128]
     wsend[...] = wrow[...].astype(BF16)
     for t in plane_partners(x, y):
         pltpu.make_async_remote_copy(
             src_ref=wsend, dst_ref=wrecv.at[xy], send_sem=sw, recv_sem=rw,
             device_id={"band": t * NZC + zc, "lev": v}, device_id_type=MESH).start()
     wrecv[xy] = wsend[...]
+    for f, g in enumerate((*winds, *synthesis((2,)))):
+        grid_o[0, f] = g
 
     pltpu.make_async_copy(wrecv.at[0 : NXY - 1], wrecv.at[0 : NXY - 1], rw).wait()
     wtab[...] = wrecv[...].astype(F32).reshape(8 * NXY, 128)
@@ -279,18 +286,24 @@
         axis=0,
     ).astype(BF16)
     lat = lax.broadcasted_iota(jnp.int32, (NXY, 128), 0) * NZC + zc
+    pl.semaphore_wait(told, NZC - 1)
     others = [lax.rem(v + d, NV) for d in (2, 1, 3, 0)]
-    for i in range(NZC):
-        g = lax.rem(zc + i, NZC)
-        for h in range(2):
-            found = jnp.dot(table, onehot[g * 2 + h], preferred_element_type=F32)
-            for j in range(2):
-                point = coup_v[g, pl.ds(2 * h + j, 1), :] >> 9
-                mine = lat == point
-                for f in range(2):
-                    picked = jnp.where(mine, found[32 * f : 32 * f + 32, 128 * j : 128 * j + 128], 0.0)
-                    line = 4 * f + 2 * h + j
-                    rrow[i, line : line + 1, :] = jnp.sum(picked, axis=0, keepdims=True)
+    bands = [lax.rem(zc + i, NZC) for i in range(NZC)]
+
+    def products(g):
+        return [jnp.dot(table, onehot[g * 2 + h], preferred_element_type=F32) for h in range(2)]
+
+    ready = products(bands[0])
+    for i, g in enumerate(bands):
+        found = ready
+        if i + 1 < NZC:
+            ready = products(bands[i + 1])
+        for line in range(4):
+            h, j = line // 2, line % 2
+            mine = lat == (coup_v[g, pl.ds(line, 1), :] >> 9)
+            for f in range(2):
+                picked = jnp.where(mine, found[h][32 * f : 32 * f + 32, 128 * j : 128 * j + 128], 0.0)
+                rrow[i, 4 * f + line : 4 * f + line + 1, :] = jnp.sum(picked, axis=0, keepdims=True)
         rsend[g] = rrow[i].astype(BF16)
         for vv in others[: 4 if i else 3]:
             pltpu.make_async_remote_copy(
@@ -396,6 +409,7 @@
             dma((5,)), dma((8,)),
             dma, dma, dma, dma, dma, dma, dma, dma,
             dma((2,)), dma((2,)), dma, dma, dma, dma,
+            pltpu.SemaphoreType.REGULAR, pltpu.SemaphoreType.REGULAR,
         ],
         compiler_params=pltpu.CompilerParams(
             collective_id=0, has_side_effects=True, vmem_limit_bytes=40 * 1024 * 1024

time: 51.7 us -> 50.1 us (0.969)
  Pallas kernels: 50.3 us -> 48.7 us
    pallas_call x1, Pallas kernels: 49.4 us -> 47.8 us  [on_device(): pl.pallas_call(kernel, out_shape=shapes, in_specs=[pl.BlockSpec(memory_sp...]
where the time goes in v4:
time: 50.1 us; the launch traced here: 50 us
  Pallas kernels  48.7 us (97%)
  between operations  1.29 us (3%)
    pallas_call x1, Pallas kernels, on_device(): pl.pallas_call(kernel, out_shape=shapes, in_specs=[pl.BlockSpec(memory_sp...  47.8 us

profile of v4, /device:TPU:1, one launch (start us, length us, event | category | flops | bytes accessed | tf_op | source)
XLA Modules:
  0.0 50.0 jit_solution(17480448489004654319)
XLA Ops:
  1.3 47.8 %shard_map.112 = (f32[1,3,1,512]{3,2,1,0:T(1,128)S(1)}, f32[9,36,4,128]{3,2,1,0:T(4,128)S(1)}, f32[4,128]{1,0:T(4,128)S(1)}) custom-call(f32[1]{0:T(128)S(6)} %copy.13.lw, bf16[15,2,1280]{2,1,0:T(2,128)(2,1)} %bitcast.6, bf16[5,256,1280]{2,1,0:T(8,128)(2,1)} %leg.1, s32[4,128]{1,0:T(4,128)} %coup.1, s32[4,128]{1,0:T(4,128)} %land.1, ...), custom_call_target="tpu_custom_call" | custom-call | tf_op jit(solution)/shard_map/pallas_call | solution.py:374
  49.1 0.9 %shard_map.113 = (f32[1,3,1,512]{3,2,1,0:T(1,128)}, f32[9,36,4,128]{3,2,1,0:T(4,128)}, f32[4,128]{1,0:T(4,128)}) custom-call(f32[1,3,1,512]{3,2,1,0:T(1,128)S(1)} %get-tuple-element.9.grid, f32[9,36,4,128]{3,2,1,0:T(4,128)S(1)} %get-tuple-element.10.out, f32[4,128]{1,0:T(4,128)S(1)} %get-tuple-element.11.char), custom_call_target="tpu_custom_call" | custom-call | tf_op jit(solution)/shard_map/pallas_call | solution.py:424

commit v5 on v4

--- a/solution.py
+++ b/solution.py
@@ -44,16 +44,16 @@
     for dy in (4, 5, 3, 6, 2, 7, 1, 0):
         yy = lax.rem(y + dy, NY)
         for xx in xs[: 4 if dy else 3]:
-            yield xx + yy
+            yield xx + yy, yy
 
 
 def kernel(
     lw, spec, leg, coup, land, spectra, cour_h, rate_h, brk_h,
     grid_o, out_o, char_o,
-    leg_v, spec_v, coup_v, land_v, own_v, s32, proj, recv1, pack, send2, recv2,
+    leg_v, spec_v, coup_v, land_v, own_v, s32, send1, recv1, pack, send2, recv2,
     rhs, ebuf, wrow, wsend, wrecv, wtab, onehot, rrow, rsend, rrecv, halo, ext, trig, state, tsum, tsend, trecv,
     cour, rate, brk,
-    leg_s, in_s, s1, r1, s2, r2, sw, rw, sr, rr, sh, rh, sc, rc, ss, rs, heard, told,
+    leg_s, in_s, s1, r1, s2, r2, sw, rw, sr, rr, sh, rh, sc, rc, ss, rs, heard, told, met, column, whole,
 ):
     b = lax.axis_index("band")
     v = lax.axis_index("lev")
@@ -76,16 +76,21 @@
     ]
     barrier = pltpu.get_barrier_semaphore()
 
-    for t in plane_partners(x, y):
-        pl.semaphore_signal(barrier, inc=1, device_id={"band": t * NZC + zc, "lev": v}, device_id_type=MESH)
+    pl.semaphore_signal(barrier, inc=1, device_id={"band": up, "lev": v}, device_id_type=MESH)
+    pl.semaphore_signal(barrier, inc=1, device_id={"band": down, "lev": v}, device_id_type=MESH)
+
+    def beside(dx, dy):
+        return (lax.rem(x + dx, NX) * NY + lax.rem(y + dy, NY)) * NZC + zc
+
+    sides = [beside(0, 1), beside(0, NY - 1), beside(1, 0), beside(NX - 1, 0)]
+    for t in sides:
+        pl.semaphore_signal(barrier, inc=1, device_id={"band": t, "lev": v}, device_id_type=MESH)
     near = [lax.rem(v + d, NV) for d in (1, NV - 1)]
     for vv in near:
         pl.semaphore_signal(barrier, inc=1, device_id={"band": b, "lev": vv}, device_id_type=MESH)
     mates = [xy * NZC + lax.rem(zc + d, NZC) for d in (4, 3, 5, 2, 6, 1, 7)]
     for t in mates:
         pl.semaphore_signal(barrier, inc=1, device_id={"band": t, "lev": v}, device_id_type=MESH)
-    pl.semaphore_signal(barrier, inc=1, device_id={"band": up, "lev": v}, device_id_type=MESH)
-    pl.semaphore_signal(barrier, inc=1, device_id={"band": down, "lev": v}, device_id_type=MESH)
 
     spec_c.start()
     for c in (*loads, coup_c, land_c, own_c, *scalars):
@@ -99,23 +104,31 @@
     held = s32[...]
     held = jnp.concatenate([held, held, held, held], axis=0)
     sm = ((sl & 31) * 43) >> 8
-    held = jnp.where((sl >> 5) == x, held, 0.0)
     acc = None
     for m in range(5):
         s_m = jnp.where(sm == m, held, 0.0).astype(BF16)
         loads[m].wait()
         d = lax.dot_general(leg_v[m], s_m, (((1,), (1,)), ((), ())), preferred_element_type=F32)
         acc = d if acc is None else acc + d
-    proj[...] = acc.reshape(NXY, 8, 128).astype(BF16)
-
-    pl.semaphore_wait(barrier, NXY - 1 + 2 + NZC - 1 + 2)
-
-    for t in plane_partners(x, y):
+    group = lax.broadcasted_iota(jnp.int32, (64, 128), 1) >> 5
+    packed = acc[0:64]
+    for i in range(1, NX):
+        packed = jnp.where(group == i, acc[64 * i : 64 * i + 64], packed)
+    pack[...] = packed
+    for j in range(NZC):
+        send1[j] = pack[pl.ds(j, NY, stride=NZC), :].astype(BF16)
+
+    pl.semaphore_wait(barrier, 4 + 2 + NZC - 1 + 2)
+
+    for d in (4, 3, 5, 2, 6, 1, 7):
+        t = lax.rem(zc + d, NZC)
         pltpu.make_async_remote_copy(
-            src_ref=proj.at[t], dst_ref=recv1.at[xy], send_sem=s1, recv_sem=r1,
-            device_id={"band": t * NZC + zc, "lev": v}, device_id_type=MESH).start()
-    recv1[xy] = proj[xy]
-
+            src_ref=send1.at[t], dst_ref=recv1.at[zc], send_sem=s1, recv_sem=r1,
+            device_id={"band": xy * NZC + t, "lev": v}, device_id_type=MESH).start()
+    recv1[zc] = send1[zc]
+
+    for t in sides:
+        pl.semaphore_signal(met, inc=1, device_id={"band": t, "lev": v}, device_id_type=MESH)
     for vv in near:
         pl.semaphore_signal(heard, inc=1, device_id={"band": b, "lev": vv}, device_id_type=MESH)
 
@@ -150,8 +163,7 @@
     rhs[0:128, LON_W:] = im_hi
     rhs[128:256, 0:LON_W] = (re - re_hi.astype(F32)).astype(BF16)
     rhs[128:256, LON_W:] = (im - im_hi.astype(F32)).astype(BF16)
-    q = lax.broadcasted_iota(jnp.int32, (64, LON_W), 0)
-    q = ((q & 7) * 8 + (q >> 3)).astype(F32)
+    q = lax.broadcasted_iota(jnp.int32, (64, LON_W), 0).astype(F32)
     lon = lax.broadcasted_iota(jnp.int32, (64, LON_W), 1).astype(F32)
     ec, es = turn(cycles(q * 5.0 * lon))
     ebuf[0] = 2.0 * ec
@@ -161,6 +173,13 @@
     trig[0] = tc
     trig[1] = ts
 
+    pl.semaphore_wait(met, 4)
+    for t in (beside(0, 2), beside(0, NY - 2)):
+        pl.semaphore_signal(column, inc=1, device_id={"band": t, "lev": v}, device_id_type=MESH)
+    pl.semaphore_wait(column, 2)
+    for d in range(1, NX):
+        pl.semaphore_signal(whole, inc=1, device_id={"band": beside(d, 0), "lev": v}, device_id_type=MESH)
+
     coup_c.wait()
     pltpu.make_async_copy(coup_v.at[0:7], coup_v.at[0:7], rc).wait()
     lon_i = lax.broadcasted_iota(jnp.int32, (LON_W, 128), 0)
@@ -174,19 +193,16 @@
 
     lax.fori_loop(0, NZC, hot, 0)
 
-    pltpu.make_async_copy(recv1.at[0 : NXY - 1], recv1.at[0 : NXY - 1], r1).wait()
+    pltpu.make_async_copy(recv1.at[0 : NZC - 1], recv1.at[0 : NZC - 1], r1).wait()
+    pack[...] = recv1[...].astype(F32).reshape(64, 128)
     for j in range(NY):
-        parts = [recv1[8 * i + j].astype(F32) for i in range(NX)]
-        pack[j * 8 : j * 8 + 8, :] = (parts[0] + parts[1]) + (parts[2] + parts[3])
-    for j in range(NZC):
-        send2[j] = pack[pl.ds(j, NY, stride=NZC), :].astype(BF16)
-
-    for j in (4, 3, 5, 2, 6, 1, 7):
-        t = lax.rem(zc + j, NZC)
+        send2[j] = pack[pl.ds(j, NZC, stride=NY), :].astype(BF16)
+    pl.semaphore_wait(whole, NX - 1)
+    for t, yy in plane_partners(x, y):
         pltpu.make_async_remote_copy(
-            src_ref=send2.at[t], dst_ref=recv2.at[zc], send_sem=s2, recv_sem=r2,
-            device_id={"band": xy * NZC + t, "lev": v}, device_id_type=MESH).start()
-    recv2[zc] = send2[zc]
+            src_ref=send2.at[yy], dst_ref=recv2.at[xy], send_sem=s2, recv_sem=r2,
+            device_id={"band": t * NZC + zc, "lev": v}, device_id_type=MESH).start()
+    recv2[xy] = send2[y]
 
     pl.semaphore_wait(heard, 2)
     for t in mates:
@@ -244,8 +260,11 @@
 
     lax.fori_loop(1, NV, send_t, 0)
 
-    pltpu.make_async_copy(recv2.at[0 : NZC - 1], recv2.at[0 : NZC - 1], r2).wait()
-    c = recv2[...].astype(F32).reshape(64, 128)
+    pltpu.make_async_copy(recv2.at[0 : NXY - 1], recv2.at[0 : NXY - 1], r2).wait()
+    c = jnp.zeros((64, 128), F32)
+    for i in range(NX):
+        part = recv2[NY * i : NY * i + NY].astype(F32).reshape(64, 128)
+        c = jnp.where(group == i, pltpu.roll(part, lax.rem(i - x + NX, NX) * 32, 1), c)
     lane = lax.broadcasted_iota(jnp.int32, (64, 128), 1)
     row = lax.broadcasted_iota(jnp.int32, (64, 128), 0)
     c = jnp.where((row == 0) & (lane < 6), 0.5 * c, c)
@@ -268,7 +287,7 @@
         for j in range(4):
             wrow[4 * f + j : 4 * f + j + 1, :] = level_weight * winds[f][:, 128 * j : 128 * j + 128]
     wsend[...] = wrow[...].astype(BF16)
-    for t in plane_partners(x, y):
+    for t, _ in plane_partners(x, y):
         pltpu.make_async_remote_copy(
             src_ref=wsend, dst_ref=wrecv.at[xy], send_sem=sw, recv_sem=rw,
             device_id={"band": t * NZC + zc, "lev": v}, device_id_type=MESH).start()
@@ -341,8 +360,8 @@
     halo_up.wait_send()
     halo_down.wait_send()
     pltpu.make_async_copy(coup_v.at[0:7], coup_v.at[0:7], sc).wait()
-    pltpu.make_async_copy(recv1.at[0 : NXY - 1], recv1.at[0 : NXY - 1], s1).wait()
-    pltpu.make_async_copy(send2.at[0 : NZC - 1], send2.at[0 : NZC - 1], s2).wait()
+    pltpu.make_async_copy(recv1.at[0 : NZC - 1], recv1.at[0 : NZC - 1], s1).wait()
+    pltpu.make_async_copy(recv2.at[0 : NXY - 1], recv2.at[0 : NXY - 1], s2).wait()
     pltpu.make_async_copy(wrecv.at[0 : NXY - 1], wrecv.at[0 : NXY - 1], sw).wait()
     pltpu.make_async_copy(rrecv.at[0 : NZ - 1], rrecv.at[0 : NZ - 1], sr).wait()
     pltpu.make_async_copy(trecv.at[0 : NV - 1], trecv.at[0 : NV - 1], ss).wait()
@@ -383,11 +402,11 @@
             pltpu.VMEM((4, 128), jnp.int32),
             pltpu.VMEM((nf, ND, 4, 128), BF16),
             pltpu.VMEM((32, N), F32),
-            pltpu.VMEM((NXY, 8, 128), BF16),
-            pltpu.VMEM((NXY, 8, 128), BF16),
-            pltpu.VMEM((64, 128), F32),
             pltpu.VMEM((NZC, 8, 128), BF16),
             pltpu.VMEM((NZC, 8, 128), BF16),
+            pltpu.VMEM((64, 128), F32),
+            pltpu.VMEM((NY, 8, 128), BF16),
+            pltpu.VMEM((NXY, 8, 128), BF16),
             pltpu.VMEM((256, 2 * LON_W), BF16),
             pltpu.VMEM((2, 64, LON_W), F32),
             pltpu.VMEM((8, 128), F32),
@@ -409,7 +428,7 @@
             dma((5,)), dma((8,)),
             dma, dma, dma, dma, dma, dma, dma, dma,
             dma((2,)), dma((2,)), dma, dma, dma, dma,
-            pltpu.SemaphoreType.REGULAR, pltpu.SemaphoreType.REGULAR,
+            *[pltpu.SemaphoreType.REGULAR] * 5,
         ],
         compiler_params=pltpu.CompilerParams(
             collective_id=0, has_side_effects=True, vmem_limit_bytes=40 * 1024 * 1024

time: 50.1 us -> 49.9 us (level)
  no operation moved by 1% of the time
where the time goes in v5:
time: 49.9 us; the launch traced here: 49.8 us
  Pallas kernels  48.5 us (97%)
  between operations  1.29 us (3%)
    pallas_call x1, Pallas kernels, on_device(): pl.pallas_call(kernel, out_shape=shapes, in_specs=[pl.BlockSpec(memory_sp...  47.6 us

profile of v5, /device:TPU:1, one launch (start us, length us, event | category | flops | bytes accessed | tf_op | source)
XLA Modules:
  0.0 49.8 jit_solution(555999755995270633)
XLA Ops:
  1.3 47.6 %shard_map.112 = (f32[1,3,1,512]{3,2,1,0:T(1,128)S(1)}, f32[9,36,4,128]{3,2,1,0:T(4,128)S(1)}, f32[4,128]{1,0:T(4,128)S(1)}) custom-call(f32[1]{0:T(128)S(6)} %copy.13.lw, bf16[15,2,1280]{2,1,0:T(2,128)(2,1)} %bitcast.6, bf16[5,256,1280]{2,1,0:T(8,128)(2,1)} %leg.1, s32[4,128]{1,0:T(4,128)} %coup.1, s32[4,128]{1,0:T(4,128)} %land.1, ...), custom_call_target="tpu_custom_call" | custom-call | tf_op jit(solution)/shard_map/pallas_call | solution.py:393
  48.9 0.9 %shard_map.113 = (f32[1,3,1,512]{3,2,1,0:T(1,128)}, f32[9,36,4,128]{3,2,1,0:T(4,128)}, f32[4,128]{1,0:T(4,128)}) custom-call(f32[1,3,1,512]{3,2,1,0:T(1,128)S(1)} %get-tuple-element.9.grid, f32[9,36,4,128]{3,2,1,0:T(4,128)S(1)} %get-tuple-element.10.out, f32[4,128]{1,0:T(4,128)S(1)} %get-tuple-element.11.char), custom_call_target="tpu_custom_call" | custom-call | tf_op jit(solution)/shard_map/pallas_call | solution.py:443

commit v6 on v5

--- a/solution.py
+++ b/solution.py
@@ -100,10 +100,8 @@
     s32[30:32, :] = jnp.zeros((2, N), F32)
     for j in range(15):
         s32[2 * j : 2 * j + 2, :] = spec_v[j].astype(F32)
-    sl = lax.broadcasted_iota(jnp.int32, (128, N), 0)
     held = s32[...]
-    held = jnp.concatenate([held, held, held, held], axis=0)
-    sm = ((sl & 31) * 43) >> 8
+    sm = (lax.broadcasted_iota(jnp.int32, (32, N), 0) * 43) >> 8
     acc = None
     for m in range(5):
         s_m = jnp.where(sm == m, held, 0.0).astype(BF16)
@@ -111,10 +109,7 @@
         d = lax.dot_general(leg_v[m], s_m, (((1,), (1,)), ((), ())), preferred_element_type=F32)
         acc = d if acc is None else acc + d
     group = lax.broadcasted_iota(jnp.int32, (64, 128), 1) >> 5
-    packed = acc[0:64]
-    for i in range(1, NX):
-        packed = jnp.where(group == i, acc[64 * i : 64 * i + 64], packed)
-    pack[...] = packed
+    pack[...] = jnp.concatenate([acc[64 * i : 64 * i + 64] for i in range(NX)], axis=1)
     for j in range(NZC):
         send1[j] = pack[pl.ds(j, NY, stride=NZC), :].astype(BF16)
 
@@ -307,7 +302,14 @@
     lat = lax.broadcasted_iota(jnp.int32, (NXY, 128), 0) * NZC + zc
     pl.semaphore_wait(told, NZC - 1)
     others = [lax.rem(v + d, NV) for d in (2, 1, 3, 0)]
-    bands = [lax.rem(zc + i, NZC) for i in range(NZC)]
+    upper = zc // 4
+    inner = lax.rem(zc // 2, 2)
+    chip = inner + upper - 2 * inner * upper
+    chips = [chip, 1 - chip, 2, 3]
+    own = lax.rem(zc, 2)
+    bands = [
+        2 * (3 * upper + (1 - 2 * upper) * t) + (own if i == 0 else 1 - own) for t in chips for i in range(2)
+    ]
 
     def products(g):
         return [jnp.dot(table, onehot[g * 2 + h], preferred_element_type=F32) for h in range(2)]

time: 49.9 us -> 50 us (level)
  no operation moved by 1% of the time
where the time goes in v6:
time: 50 us; the launch traced here: 49.9 us
  Pallas kernels  48.6 us (97%)
  between operations  1.29 us (3%)
    pallas_call x1, Pallas kernels, on_device(): pl.pallas_call(kernel, out_shape=shapes, in_specs=[pl.BlockSpec(memory_sp...  47.7 us

profile of v6, /device:TPU:1, one launch (start us, length us, event | category | flops | bytes accessed | tf_op | source)
XLA Modules:
  0.0 49.9 jit_solution(12122305122353969589)
XLA Ops:
  1.3 47.7 %shard_map.112 = (f32[1,3,1,512]{3,2,1,0:T(1,128)S(1)}, f32[9,36,4,128]{3,2,1,0:T(4,128)S(1)}, f32[4,128]{1,0:T(4,128)S(1)}) custom-call(f32[1]{0:T(128)S(6)} %copy.13.lw, bf16[15,2,1280]{2,1,0:T(2,128)(2,1)} %bitcast.6, bf16[5,256,1280]{2,1,0:T(8,128)(2,1)} %leg.1, s32[4,128]{1,0:T(4,128)} %coup.1, s32[4,128]{1,0:T(4,128)} %land.1, ...), custom_call_target="tpu_custom_call" | custom-call | tf_op jit(solution)/shard_map/pallas_call | solution.py:395
  49.0 0.9 %shard_map.113 = (f32[1,3,1,512]{3,2,1,0:T(1,128)}, f32[9,36,4,128]{3,2,1,0:T(4,128)}, f32[4,128]{1,0:T(4,128)}) custom-call(f32[1,3,1,512]{3,2,1,0:T(1,128)S(1)} %get-tuple-element.9.grid, f32[9,36,4,128]{3,2,1,0:T(4,128)S(1)} %get-tuple-element.10.out, f32[4,128]{1,0:T(4,128)S(1)} %get-tuple-element.11.char), custom_call_target="tpu_custom_call" | custom-call | tf_op jit(solution)/shard_map/pallas_call | solution.py:445
